TPU v7x, 32 devices: a whole 2x2x4 slice. The times are simulated.
32 devices in a mesh: dom: 8 (over z, x), mp: 4 (over y, core).
Axes of the slice: x: 2, y: 2, z: 4, core: 2. Of those that a mesh axis runs over, the one named last changes fastest.
Arguments:
- node_states: bfloat16 [2048, 1024], P(('dom', 'mp')), may hold values from -6 to 6
- edge_states: bfloat16 [6144, 1024], P(('dom', 'mp')), may hold values from -6 to 6
- edge_weight: bfloat16 [1024, 1024], P('mp'), may hold values from -0.109375 to 0.109375
- send_weight: bfloat16 [1024, 1024], P('mp'), may hold values from -0.109375 to 0.109375
- receive_weight: bfloat16 [1024, 1024], P('mp'), may hold values from -0.109375 to 0.109375
- output_weight: bfloat16 [1024, 1024], P('mp'), may hold values from -0.1875 to 0.1875
- norm_gain: float32 [1024], replicated, may hold values from 0.5 to 1.5
- senders: int32 [6144], P(('dom', 'mp')), may hold values from 0 to 127
- receivers: int32 [6144], P(('dom', 'mp')), may hold values from 0 to 63
- send_rows: int32 [32, 4, 16], P(('dom', 'mp')), may hold values from 0 to 63
- node_cotangent: bfloat16 [2048, 1024], P(('dom', 'mp')), may hold values from -6 to 6
- edge_cotangent: bfloat16 [6144, 1024], P(('dom', 'mp')), may hold values from -6 to 6
Outputs:
- new_nodes: bfloat16 [2048, 1024], P(('dom', 'mp'))
- new_edges: bfloat16 [6144, 1024], P(('dom', 'mp'))
- grad_nodes: bfloat16 [2048, 1024], P(('dom', 'mp'))
- grad_edges: bfloat16 [6144, 1024], P(('dom', 'mp'))
Inputs may be any that keep to these rules, and one draw needn't show every extreme that they name: `senders`: A table row of the edge's own block. `receivers`: A node of the edge's own block. `send_rows`: local node indices of the sending block; a node may be listed more than once.
All inputs are finite; a program needn't handle non-finite values.
Results may differ from a plain program's by a relative error of at most 0.0059.
Values may be sent and summed in bfloat16 or wider, within the bound.
A program may use at most 64 MiB of HBM per device.

v0:
```python
import jax
import jax.numpy as jnp
from jax import lax
from jax.sharding import PartitionSpec as P

eps = 1e-05


def shifted(value, axis, steps):
    count = lax.axis_size(axis)
    pairs = [(source, (source + steps) % count) for source in range(count)]
    return lax.ppermute(value, axis, pairs)


def normalize(values, norm_gain):
    average = jnp.mean(values, axis=-1, keepdims=True)
    centred = values - average
    variance = jnp.mean(centred * centred, axis=-1, keepdims=True)
    return centred * lax.rsqrt(variance + eps) * norm_gain


def silu_slope(preact):
    sigmoid_value = jax.nn.sigmoid(preact)
    return sigmoid_value * (1.0 + preact * (1.0 - sigmoid_value))


def product(left, right):
    return jnp.dot(left, right, preferred_element_type=jnp.float32)


def rows_product(left, right):
    return lax.dot_general(
        left, right, (((1,), (1,)), ((), ())), preferred_element_type=jnp.float32
    )


def send_out(block, stride):
    return shifted(block, ("dom", "mp"), stride)


def send_back(block, stride):
    return shifted(block, ("dom", "mp"), stride)


def shards(
    node_states,
    edge_states,
    edge_weight,
    send_weight,
    receive_weight,
    output_weight,
    norm_gain,
    senders,
    receivers,
    send_rows,
    node_cotangent,
    edge_cotangent,
):
    node_count = node_states.shape[0]
    spread = send_rows.shape[1] // 2
    halo_rows = send_rows.shape[2]
    shifts = [stride + 1 for stride in range(spread)] + [-(stride + 1) for stride in range(spread)]
    chosen_rows = send_rows[0]

    def collect(source):
        arrived = [
            send_out(jnp.take(source, chosen_rows[block_index], axis=0), shifts[block_index])
            for block_index in range(2 * spread)
        ]
        return jnp.concatenate([source] + arrived, axis=0)

    output_full = lax.all_gather(output_weight, "mp", axis=0, tiled=True)
    edge_full, send_full, receive_full = (
        lax.all_gather(edge_weight, "mp", axis=0, tiled=True),
        lax.all_gather(send_weight, "mp", axis=0, tiled=True),
        lax.all_gather(receive_weight, "mp", axis=0, tiled=True),
    )
    edge_part = product(edge_states, edge_full)
    send_projection = product(node_states, send_full)
    receive_projection = product(node_states, receive_full)
    send_projection = send_projection.astype(jnp.bfloat16)
    receive_projection = receive_projection.astype(jnp.bfloat16)
    lookup = collect(send_projection)
    preact = edge_part + jnp.take(lookup, senders, axis=0).astype(jnp.float32)
    preact = preact + jnp.take(receive_projection, receivers, axis=0).astype(jnp.float32)
    hidden = jax.nn.silu(preact).astype(jnp.bfloat16)
    projected = product(hidden, output_full)

    def apply_norm(values):
        return normalize(values, norm_gain)

    update, norm_back = jax.vjp(apply_norm, projected)
    new_edges = (edge_states.astype(jnp.float32) + update).astype(jnp.bfloat16)
    summed = jax.ops.segment_sum(new_edges.astype(jnp.float32), receivers, num_segments=node_count)
    new_nodes = (node_states.astype(jnp.float32) + summed).astype(jnp.bfloat16)
    grad_total = edge_cotangent.astype(jnp.float32) + jnp.take(
        node_cotangent, receivers, axis=0
    ).astype(jnp.float32)
    grad_projected = norm_back(grad_total)[0].astype(jnp.bfloat16)
    grad_hidden = rows_product(grad_projected, output_full)
    grad_preact = (grad_hidden * silu_slope(preact)).astype(jnp.bfloat16)
    grad_lookup = jax.ops.segment_sum(
        grad_preact.astype(jnp.float32), senders, num_segments=lookup.shape[0]
    )
    grad_receive = jax.ops.segment_sum(
        grad_preact.astype(jnp.float32), receivers, num_segments=node_count
    ).astype(jnp.bfloat16)
    grad_send = grad_lookup[:node_count]
    for block_index in range(2 * spread):
        start_row = node_count + block_index * halo_rows
        returned = send_back(
            grad_lookup[start_row : start_row + halo_rows].astype(jnp.bfloat16),
            -shifts[block_index],
        )
        grad_send = grad_send.at[chosen_rows[block_index]].add(returned.astype(jnp.float32))
    grad_send = grad_send.astype(jnp.bfloat16)
    grad_edge_part = rows_product(grad_preact, edge_full)
    grad_node_part = rows_product(grad_send, send_full) + rows_product(grad_receive, receive_full)
    grad_edges = (grad_total + grad_edge_part).astype(jnp.bfloat16)
    grad_nodes = (node_cotangent.astype(jnp.float32) + grad_node_part).astype(jnp.bfloat16)
    return (new_nodes, new_edges, grad_nodes, grad_edges)


def solution(mesh):
    in_specs = (
        P(("dom", "mp"), None),
        P(("dom", "mp"), None),
        P("mp", None),
        P("mp", None),
        P("mp", None),
        P("mp", None),
        P(),
        P(("dom", "mp")),
        P(("dom", "mp")),
        P(("dom", "mp"), None, None),
        P(("dom", "mp"), None),
        P(("dom", "mp"), None),
    )
    out_specs = (
        P(("dom", "mp"), None),
        P(("dom", "mp"), None),
        P(("dom", "mp"), None),
        P(("dom", "mp"), None),
    )
    return jax.shard_map(shards, mesh=mesh, in_specs=in_specs, out_specs=out_specs, check_vma=False)
```

profile of v0, /device:TPU:0, one launch (start us, length us, event | category | flops | bytes accessed | tf_op | source)
XLA Modules:
  0.0 154.4 jit_solution(8180012247334045418)
XLA Ops:
  7.2 0.0 all-gather.7.cloned.1.call-start
  7.3 0.7 all-gather.7.cloned.1.call-update
  8.0 0.0 all-gather.5.cloned.1.call-start
  8.0 0.7 all-gather.5.cloned.1.call-update
  8.7 0.0 all-gather.9.cloned.1.call-start
  8.7 0.7 all-gather.9.cloned.1.call-update
  9.4 0.0 all-gather.11.cloned.1.call-start
  9.5 0.5 all-gather.11.cloned.1.call-update
  10.1 0.7 convert_element_type.77
  10.9 1.0 gather_fusion.6
  11.9 0.0 copy-start.3
  12.0 0.0 copy-start.15
  12.0 0.6 fusion.31
  12.6 22.3 %all-gather.7.cloned.1.call-done = bf16[1024,1024]{1,0:T(8,128)(2,1)} async-done(((bf16[256,1024]{1,0:T(8,128)(2,1)}), bf16[1024,1024]{1,0:T(8,128)(2,1)}) %all-gather.7.cloned.1.call-update) | async-done | bytes 2097168 | tf_op jit(solution)/shard_map/all_gather | solution.py:75
  34.9 2.1 %constant_dynamic-update-slice_fusion.4 = (bf16[128,1024]{1,0:T(8,128)(2,1)S(1)}, bf16[64,1024]{1,0:T(8,128)(2,1)S(1)}) fusion(bf16[64,1024]{1,0:T(8,128)(2,1)S(1)} %copy-done.6, bf16[1024,1024]{1,0:T(8,128)(2,1)} %all-gather.7.cloned.1.call-done), kind=kOutput, calls=%fused_computation.64 | convolution fusion | flops 134283264 | bytes 2490368 | tf_op jit(solution)/shard_map/dot_general | solution.py:28
  37.0 0.6 gather_fusion.1
  37.6 0.1 broadcast_select_fusion.4
  37.7 0.2 collective-permute-start
  37.9 0.6 gather_fusion.2
  38.5 0.1 broadcast_select_fusion.3
  38.6 0.3 collective-permute-start.1
  38.9 0.6 gather_fusion.3
  39.5 0.1 broadcast_select_fusion.2
  39.6 4.8 %collective-permute-start.2 = (bf16[16,1024]{1,0:T(8,128)(2,1)S(1)}, bf16[16,1024]{1,0:T(8,128)(2,1)S(1)}, u32[]{:S(2)}, u32[]{:S(2)}) collective-permute-start(bf16[16,1024]{1,0:T(8,128)(2,1)S(1)} %broadcast_select_fusion.2), channel_id=1, source_target_pairs={{0,31},{1,0},{2,1},{3,2},{4,3},{5,4},{6,5},{7,6},{8,7},{9,8},{10,9... | collective-permute-start | bytes 98312 | tf_op jit(solution)/shard_map/ppermute | solution.py:12
  44.4 0.6 gather_fusion.4
  45.0 0.1 broadcast_select_fusion.1
  45.1 1.7 %collective-permute-start.3 = (bf16[16,1024]{1,0:T(8,128)(2,1)S(1)}, bf16[16,1024]{1,0:T(8,128)(2,1)S(1)}, u32[]{:S(2)}, u32[]{:S(2)}) collective-permute-start(bf16[16,1024]{1,0:T(8,128)(2,1)S(1)} %broadcast_select_fusion.1), channel_id=1, source_target_pairs={{0,30},{1,31},{2,0},{3,1},{4,2},{5,3},{6,4},{7,5},{8,6},{9,7},{10,... | collective-permute-start | bytes 98312 | tf_op jit(solution)/shard_map/ppermute | solution.py:12
  46.8 12.7 %all-gather.5.cloned.1.call-done = bf16[1024,1024]{1,0:T(8,128)(2,1)} async-done(((bf16[256,1024]{1,0:T(8,128)(2,1)}), bf16[1024,1024]{1,0:T(8,128)(2,1)}) %all-gather.5.cloned.1.call-update) | async-done | bytes 2097168 | tf_op jit(solution)/shard_map/all_gather | solution.py:74
  59.5 2.2 %fusion.36 = f32[192,1024]{1,0:T(8,128)S(1)} fusion(bf16[192,1024]{1,0:T(8,128)(2,1)S(1)} %copy-done.3, bf16[1024,1024]{1,0:T(8,128)(2,1)} %all-gather.5.cloned.1.call-done), kind=kOutput, calls=%fused_computation.100 | convolution fusion | flops 402653184 | bytes 3276800 | tf_op jit(solution)/shard_map/dot_general | solution.py:28
  61.7 22.7 %all-gather.9.cloned.1.call-done = bf16[1024,1024]{1,0:T(8,128)(2,1)} async-done(((bf16[256,1024]{1,0:T(8,128)(2,1)}), bf16[1024,1024]{1,0:T(8,128)(2,1)}) %all-gather.9.cloned.1.call-update) | async-done | bytes 2097168 | tf_op jit(solution)/shard_map/all_gather | solution.py:76
  84.3 2.1 %convolution_convert_fusion = bf16[64,1024]{1,0:T(8,128)(2,1)S(1)} fusion(bf16[64,1024]{1,0:T(8,128)(2,1)S(1)} %copy-done.6, bf16[1024,1024]{1,0:T(8,128)(2,1)} %all-gather.9.cloned.1.call-done), kind=kOutput, calls=%fused_computation.22 | convolution fusion | flops 134283264 | bytes 2359296 | tf_op jit(solution)/shard_map/dot_general | solution.py:28
  86.4 1.0 gather_fusion.5
  87.4 0.0 collective-permute-done
  87.5 0.0 collective-permute-done.1
  87.5 1.0 gather_fusion
  88.6 0.0 copy-start.8
  88.6 0.0 copy-start.5
  88.6 0.0 copy-start.10
  88.6 19.8 %all-gather.11.cloned.1.call-done = bf16[1024,1024]{1,0:T(8,128)(2,1)} async-done(((bf16[256,1024]{1,0:T(8,128)(2,1)}), bf16[1024,1024]{1,0:T(8,128)(2,1)}) %all-gather.11.cloned.1.call-update) | async-done | bytes 2097168 | tf_op jit(solution)/shard_map/all_gather | solution.py:72
  108.4 2.5 %fusion.35 = (f32[192]{0:T(256)S(1)}, f32[192,1024]{1,0:T(8,128)S(1)}) fusion(bf16[1024,1024]{1,0:T(8,128)(2,1)} %all-gather.11.cloned.1.call-done, bf16[192,1024]{1,0:T(8,128)(2,1)S(1)} %gather_fusion.5, pred[192]{0:T(512)(128)(4,1)S(1)} %compare_and_fusion, f32[192,1024]{1,0:T(8,128)S(1)} %fusion.36, bf16[192,1024]{1,0:T(8,128)(2,1)S(1)} %gather_fusion, ...), kind=kOutput, calls=%fused_computation.99 | convolution fusion | flops 405012288 | bytes 4457600 | tf_op jit(solution)/shard_map/dot_general | solution.py:28
  110.9 0.0 copy-start.9
  110.9 0.0 copy-start.16
  110.9 0.4 multiply_reduce_fusion
  111.4 0.6 fusion.33
  112.0 0.6 copy-done.14
  112.6 1.0 fusion
  113.7 2.3 %scatter_custom_fusion.1 = f32[128,1024]{1,0:T(8,128)S(1)} fusion(s32[192]{0:T(256)S(1)} %copy-done.12, bf16[192,1024]{1,0:T(8,128)(2,1)S(1)} %fusion, f32[]{:T(128)} %constant.36.clone.1), kind=kCustom, calls=%fused_computation.26 | custom fusion | flops 393216 | bytes 917508 | tf_op jit(solution)/shard_map/scatter-add | solution.py:102
  116.0 2.2 %scatter_custom_fusion.6 = f32[64,1024]{1,0:T(8,128)S(1)} fusion(s32[192]{0:T(256)S(1)} %copy-done.13, bf16[192,1024]{1,0:T(8,128)(2,1)S(1)} %fusion, f32[]{:T(128)} %constant.36.clone.1), kind=kCustom, calls=%fused_computation.24 | custom fusion | flops 393216 | bytes 655364 | tf_op jit(solution)/shard_map/scatter-add | solution.py:105
  118.3 0.6 fusion.34
  118.9 4.1 %collective-permute-start.4 = (bf16[16,1024]{1,0:T(8,128)(2,1)}, bf16[16,1024]{1,0:T(8,128)(2,1)S(1)}, u32[]{:S(2)}, u32[]{:S(2)}) collective-permute-start(bf16[16,1024]{1,0:T(8,128)(2,1)} %get-tuple-element.22), channel_id=1, source_target_pairs={{0,31},{1,0},{2,1},{3,2},{4,3},{5,4},{6,5},{7,6},{8,7},{9,8},{10,9... | collective-permute-start | bytes 98312 | tf_op jit(solution)/shard_map/ppermute | solution.py:12
  123.0 1.5 collective-permute-start.5
  124.5 0.0 collective-permute-start.6
  124.5 0.6 collective-permute-start.7
  125.0 3.2 %fusion.1 = bf16[192,1024]{1,0:T(8,128)(2,1)} fusion(bf16[192,1024]{1,0:T(8,128)(2,1)S(1)} %fusion, bf16[1024,1024]{1,0:T(8,128)(2,1)} %all-gather.5.cloned.1.call-done, bf16[192,1024]{1,0:T(8,128)(2,1)S(1)} %copy-done.5, bf16[192,1024]{1,0:T(8,128)(2,1)S(1)} %gather_fusion.6, pred[192]{0:T(512)(128)(4,1)S(1)} %compare_and_fusion), kind=kOutput, calls=%fused_computation.17 | convolution fusion | flops 403832832 | bytes 3670208 | tf_op jit(solution)/shard_map/dot_general | solution.py:32
  128.2 1.5 fusion.15
  129.7 0.7 slice.62
  130.4 3.8 %scatter_custom_fusion = f32[64,1024]{1,0:T(8,128)} fusion(f32[64,1024]{1,0:T(8,128)} %convert_element_type.77, s32[192]{0:T(256)S(1)} %copy-done.13, bf16[192,1024]{1,0:T(8,128)(2,1)S(1)} %get-tuple-element.18), kind=kCustom, calls=%fused_computation.31 | custom fusion | flops 393216 | bytes 655360 | tf_op jit(solution)/shard_map/scatter-add | solution.py:94
  134.2 1.6 %convert_element_type.86 = bf16[64,1024]{1,0:T(8,128)(2,1)} convert(f32[64,1024]{1,0:T(8,128)} %scatter_custom_fusion) | non-fusion elementwise | flops 65536 | bytes 393216 | tf_op jit(solution)/shard_map/convert_element_type | solution.py:95
  135.8 2.4 %scatter_custom_fusion.2 = f32[64,1024]{1,0:T(8,128)} fusion(f32[64,1024]{1,0:T(8,128)} %slice.62, s32[16]{0:T(128)} %get-tuple-element.24, bf16[16,1024]{1,0:T(8,128)(2,1)S(1)} %collective-permute-done.4), kind=kCustom, calls=%fused_computation.54 | custom fusion | flops 32768 | bytes 294912 | tf_op jit(solution)/shard_map/scatter-add | solution.py:115
  138.3 2.4 %scatter_custom_fusion.3 = f32[64,1024]{1,0:T(8,128)} fusion(f32[64,1024]{1,0:T(8,128)} %scatter_custom_fusion.2, s32[16]{0:T(128)} %get-tuple-element.25, bf16[16,1024]{1,0:T(8,128)(2,1)S(1)} %collective-permute-done.5), kind=kCustom, calls=%fused_computation.52 | custom fusion | flops 32768 | bytes 294912 | tf_op jit(solution)/shard_map/scatter-add | solution.py:115
  140.7 0.0 collective-permute-done.6
  140.7 2.4 %scatter_custom_fusion.4 = f32[64,1024]{1,0:T(8,128)} fusion(f32[64,1024]{1,0:T(8,128)} %scatter_custom_fusion.3, s32[16]{0:T(128)} %get-tuple-element.26, bf16[16,1024]{1,0:T(8,128)(2,1)S(1)} %collective-permute-done.6), kind=kCustom, calls=%fused_computation.50 | custom fusion | flops 32768 | bytes 294912 | tf_op jit(solution)/shard_map/scatter-add | solution.py:115
  143.2 2.3 %scatter_custom_fusion.5 = f32[64,1024]{1,0:T(8,128)} fusion(f32[64,1024]{1,0:T(8,128)} %scatter_custom_fusion.4, s32[16]{0:T(128)S(1)} %get-tuple-element.23, bf16[16,1024]{1,0:T(8,128)(2,1)S(1)} %collective-permute-done.7), kind=kCustom, calls=%fused_computation.48 | custom fusion | flops 32768 | bytes 294912 | tf_op jit(solution)/shard_map/scatter-add | solution.py:115
  145.5 2.4 %fusion.3 = bf16[64,1024]{1,0:T(8,128)(2,1)} fusion(f32[64,1024]{1,0:T(8,128)S(1)} %copy-done.7, bf16[1024,1024]{1,0:T(8,128)(2,1)S(1)} %copy-done.2, bf16[64,1024]{1,0:T(8,128)(2,1)S(1)} %copy-done, f32[64,1024]{1,0:T(8,128)} %scatter_custom_fusion.5), kind=kOutput, calls=%fused_computation.21 | convolution fusion | flops 134545408 | bytes 2883584 | tf_op jit(solution)/shard_map/dot_general | solution.py:32
  (49 shorter events, 0.2 us)
Async XLA Ops:
  7.2 2.8 %copy-start.11 = (s32[1,4,16]{2,1,0:T(4,128)S(1)}, s32[1,4,16]{2,1,0:T(4,128)}, u32[]{:S(2)}) copy-start(s32[1,4,16]{2,1,0:T(4,128)} %param.25) | copy-start | bytes 772
  7.2 2.9 %copy-start.13 = (s32[192]{0:T(256)S(1)}, s32[192]{0:T(256)}, u32[]{:S(2)}) copy-start(s32[192]{0:T(256)} %param.24) | copy-start | bytes 2308
  7.2 2.9 %copy-start.12 = (s32[192]{0:T(256)S(1)}, s32[192]{0:T(256)}, u32[]{:S(2)}) copy-start(s32[192]{0:T(256)} %param.23) | copy-start | bytes 2308
  7.2 2.9 %copy-start.6 = (bf16[64,1024]{1,0:T(8,128)(2,1)S(1)}, bf16[64,1024]{1,0:T(8,128)(2,1)}, u32[]{:S(2)}) copy-start(bf16[64,1024]{1,0:T(8,128)(2,1)} %param.16) | copy-start | bytes 393220
  7.2 3.7 %copy-start = (bf16[64,1024]{1,0:T(8,128)(2,1)S(1)}, bf16[64,1024]{1,0:T(8,128)(2,1)}, u32[]{:S(2)}) copy-start(bf16[64,1024]{1,0:T(8,128)(2,1)} %param.26) | copy-start | bytes 393220
  7.2 27.7 %all-gather.7.cloned.1.call-start = ((), (), s32[]{:S(2)}) async-start(), calls=%async_computation.1 | async-start | bytes 2621440 | tf_op jit(solution)/shard_map/all_gather | solution.py:75
  8.0 51.5 %all-gather.5.cloned.1.call-start = ((), (), s32[]{:S(2)}) async-start(), calls=%async_computation | async-start | bytes 2621440 | tf_op jit(solution)/shard_map/all_gather | solution.py:74
  8.7 75.6 %all-gather.9.cloned.1.call-start = ((), (), s32[]{:S(2)}) async-start(), calls=%async_computation.2 | async-start | bytes 2621440 | tf_op jit(solution)/shard_map/all_gather | solution.py:76
  9.4 98.9 %all-gather.11.cloned.1.call-start = ((), (), s32[]{:S(2)}) async-start(), calls=%async_computation.3 | async-start | bytes 2621440 | tf_op jit(solution)/shard_map/all_gather | solution.py:72
  11.9 47.6 %copy-start.3 = (bf16[192,1024]{1,0:T(8,128)(2,1)S(1)}, bf16[192,1024]{1,0:T(8,128)(2,1)}, u32[]{:S(2)}) copy-start(bf16[192,1024]{1,0:T(8,128)(2,1)} %param.17) | copy-start | bytes 1179652
  12.0 96.4 %copy-start.15 = (pred[192]{0:T(512)(128)(4,1)}, pred[192]{0:T(512)(128)(4,1)S(1)}, u32[]{:S(2)}) copy-start(pred[192]{0:T(512)(128)(4,1)S(1)} %compare_and_fusion.5) | copy-start | bytes 580
  37.7 49.8 %collective-permute-start = (bf16[16,1024]{1,0:T(8,128)(2,1)S(1)}, bf16[16,1024]{1,0:T(8,128)(2,1)S(1)}, u32[]{:S(2)}, u32[]{:S(2)}) collective-permute-start(bf16[16,1024]{1,0:T(8,128)(2,1)S(1)} %broadcast_select_fusion.4), channel_id=1, source_target_pairs={{0,1},{1,2},{2,3},{3,4},{4,5},{5,6},{6,7},{7,8},{8,9},{9,10},{10,1... | collective-permute-start | bytes 98312 | tf_op jit(solution)/shard_map/ppermute | solution.py:12
  38.6 48.9 %collective-permute-start.1 = (bf16[16,1024]{1,0:T(8,128)(2,1)S(1)}, bf16[16,1024]{1,0:T(8,128)(2,1)S(1)}, u32[]{:S(2)}, u32[]{:S(2)}) collective-permute-start(bf16[16,1024]{1,0:T(8,128)(2,1)S(1)} %broadcast_select_fusion.3), channel_id=1, source_target_pairs={{0,2},{1,3},{2,4},{3,5},{4,6},{5,7},{6,8},{7,9},{8,10},{9,11},{10,... | collective-permute-start | bytes 98312 | tf_op jit(solution)/shard_map/ppermute | solution.py:12
  39.6 47.9 %collective-permute-start.2 = (bf16[16,1024]{1,0:T(8,128)(2,1)S(1)}, bf16[16,1024]{1,0:T(8,128)(2,1)S(1)}, u32[]{:S(2)}, u32[]{:S(2)}) collective-permute-start(bf16[16,1024]{1,0:T(8,128)(2,1)S(1)} %broadcast_select_fusion.2), channel_id=1, source_target_pairs={{0,31},{1,0},{2,1},{3,2},{4,3},{5,4},{6,5},{7,6},{8,7},{9,8},{10,9... | collective-permute-start | bytes 98312 | tf_op jit(solution)/shard_map/ppermute | solution.py:12
  45.1 42.4 %collective-permute-start.3 = (bf16[16,1024]{1,0:T(8,128)(2,1)S(1)}, bf16[16,1024]{1,0:T(8,128)(2,1)S(1)}, u32[]{:S(2)}, u32[]{:S(2)}) collective-permute-start(bf16[16,1024]{1,0:T(8,128)(2,1)S(1)} %broadcast_select_fusion.1), channel_id=1, source_target_pairs={{0,30},{1,31},{2,0},{3,1},{4,2},{5,3},{6,4},{7,5},{8,6},{9,7},{10,... | collective-permute-start | bytes 98312 | tf_op jit(solution)/shard_map/ppermute | solution.py:12
  88.6 22.3 %copy-start.8 = (bf16[192,1024]{1,0:T(8,128)(2,1)}, bf16[192,1024]{1,0:T(8,128)(2,1)S(1)}, u32[]{:S(2)}) copy-start(bf16[192,1024]{1,0:T(8,128)(2,1)S(1)} %gather_fusion) | copy-start | bytes 1179652
  88.6 22.3 %copy-start.5 = (bf16[192,1024]{1,0:T(8,128)(2,1)S(1)}, bf16[192,1024]{1,0:T(8,128)(2,1)}, u32[]{:S(2)}) copy-start(bf16[192,1024]{1,0:T(8,128)(2,1)} %param.27) | copy-start | bytes 1179652
  88.6 22.3 %copy-start.10 = (f32[1024]{0:T(1024)S(1)}, f32[1024]{0:T(1024)}, u32[]{:S(2)}) copy-start(f32[1024]{0:T(1024)} %param.22) | copy-start | bytes 12292
  110.9 1.2 copy-start.9
  110.9 1.7 %copy-start.14 = (bf16[1024,1024]{1,0:T(8,128)(2,1)S(1)}, bf16[1024,1024]{1,0:T(8,128)(2,1)}, u32[]{:S(2)}) copy-start(bf16[1024,1024]{1,0:T(8,128)(2,1)} %all-gather.11.cloned.1.call-done) | copy-start | bytes 6291460
  110.9 1.7 %copy-start.16 = (pred[192]{0:T(512)(128)(4,1)S(1)}, pred[192]{0:T(512)(128)(4,1)}, u32[]{:S(2)}) copy-start(pred[192]{0:T(512)(128)(4,1)} %copy-done.15) | copy-start | bytes 580
  112.0 18.4 %copy-start.4 = (bf16[192,1024]{1,0:T(8,128)(2,1)}, bf16[192,1024]{1,0:T(8,128)(2,1)S(1)}, u32[]{:S(2)}) copy-start(bf16[192,1024]{1,0:T(8,128)(2,1)S(1)} %get-tuple-element.18) | copy-start | bytes 1179652
  118.3 10.0 %copy-start.1 = (bf16[1024,1024]{1,0:T(8,128)(2,1)S(1)}, bf16[1024,1024]{1,0:T(8,128)(2,1)}, u32[]{:S(2)}) copy-start(bf16[1024,1024]{1,0:T(8,128)(2,1)} %all-gather.9.cloned.1.call-done) | copy-start | bytes 6291460
  118.9 16.9 %collective-permute-start.4 = (bf16[16,1024]{1,0:T(8,128)(2,1)}, bf16[16,1024]{1,0:T(8,128)(2,1)S(1)}, u32[]{:S(2)}, u32[]{:S(2)}) collective-permute-start(bf16[16,1024]{1,0:T(8,128)(2,1)} %get-tuple-element.22), channel_id=1, source_target_pairs={{0,31},{1,0},{2,1},{3,2},{4,3},{5,4},{6,5},{7,6},{8,7},{9,8},{10,9... | collective-permute-start | bytes 98312 | tf_op jit(solution)/shard_map/ppermute | solution.py:12
  123.0 15.3 %collective-permute-start.5 = (bf16[16,1024]{1,0:T(8,128)(2,1)}, bf16[16,1024]{1,0:T(8,128)(2,1)S(1)}, u32[]{:S(2)}, u32[]{:S(2)}) collective-permute-start(bf16[16,1024]{1,0:T(8,128)(2,1)} %get-tuple-element.21), channel_id=1, source_target_pairs={{0,30},{1,31},{2,0},{3,1},{4,2},{5,3},{6,4},{7,5},{8,6},{9,7},{10,... | collective-permute-start | bytes 98312 | tf_op jit(solution)/shard_map/ppermute | solution.py:12
  124.5 16.3 %collective-permute-start.6 = (bf16[16,1024]{1,0:T(8,128)(2,1)}, bf16[16,1024]{1,0:T(8,128)(2,1)S(1)}, u32[]{:S(2)}, u32[]{:S(2)}) collective-permute-start(bf16[16,1024]{1,0:T(8,128)(2,1)} %get-tuple-element.20), channel_id=1, source_target_pairs={{0,1},{1,2},{2,3},{3,4},{4,5},{5,6},{6,7},{7,8},{8,9},{9,10},{10,1... | collective-permute-start | bytes 98312 | tf_op jit(solution)/shard_map/ppermute | solution.py:12
  124.5 18.7 %collective-permute-start.7 = (bf16[16,1024]{1,0:T(8,128)(2,1)}, bf16[16,1024]{1,0:T(8,128)(2,1)S(1)}, u32[]{:S(2)}, u32[]{:S(2)}) collective-permute-start(bf16[16,1024]{1,0:T(8,128)(2,1)} %get-tuple-element.19), channel_id=1, source_target_pairs={{0,2},{1,3},{2,4},{3,5},{4,6},{5,7},{6,8},{7,9},{8,10},{9,11},{10,... | collective-permute-start | bytes 98312 | tf_op jit(solution)/shard_map/ppermute | solution.py:12
  128.2 17.2 %copy-start.2 = (bf16[1024,1024]{1,0:T(8,128)(2,1)S(1)}, bf16[1024,1024]{1,0:T(8,128)(2,1)}, u32[]{:S(2)}) copy-start(bf16[1024,1024]{1,0:T(8,128)(2,1)} %all-gather.7.cloned.1.call-done) | copy-start | bytes 6291460
  129.7 15.8 %copy-start.7 = (f32[64,1024]{1,0:T(8,128)S(1)}, f32[64,1024]{1,0:T(8,128)}, u32[]{:S(2)}) copy-start(f32[64,1024]{1,0:T(8,128)} %fusion.15) | copy-start | bytes 786436
Sparse Core Ops, SparseCore 0:
  9.6 25.2 all-gather.6
  36.5 22.9 all-gather.4
  61.1 23.2 all-gather.8
  85.8 22.5 all-gather.10
where the time goes:
time: 155 us; the launch traced here: 154 us
  waiting for transfers between devices  80.1 us (52%)
  other arithmetic  22.4 us (14%)
  matrix products  16.8 us (11%)
  between operations  14.2 us (9%)
  starting transfers between devices  13.4 us (9%)
  local copies, waits for them, and re-layouts  7.43 us (5%)
    all_gather x1, waiting for transfers between devices, shards(): lax.all_gather(receive_weight, 'mp', axis=0, tiled=True)  22.7 us
    all_gather x1, waiting for transfers between devices, shards(): lax.all_gather(send_weight, 'mp', axis=0, tiled=True)  22.3 us
    all_gather x1, waiting for transfers between devices, shards(): output_full = lax.all_gather(output_weight, 'mp', axis=0, tiled=True)  19.8 us
    ppermute x8, starting transfers between devices, shifted(): return lax.ppermute(value, axis, pairs)  13.2 us
    all_gather x1, waiting for transfers between devices, shards(): lax.all_gather(edge_weight, 'mp', axis=0, tiled=True)  12.7 us
    scatter-add x4, other arithmetic, shards(): grad_send.at[chosen_rows[block_index]].add(returned.astype(jnp.float32))  9.63 us
    dot_general x4, matrix products, product(): return jnp.dot(left, right, preferred_element_type=jnp.float32)  8.76 us
    dot_general x4, matrix products, rows_product(): lax.dot_general(left, right, (((1,), (1,)), ((), ())), preferred_element_...  8.08 us
  transfers between devices with their start and end apart: 12, of which 4 were waited for; matrix products, arithmetic and copies ran while one was open for 20% of the time, Pallas kernels for 0%

commit v1 on v0

v1 whole, which is shorter than its diff:
```python
import functools

import jax
import jax.numpy as jnp
from jax import lax
from jax.experimental import pallas as pl
from jax.experimental.pallas import tpu as pltpu
from jax.sharding import PartitionSpec as P

eps = 1e-05
MESH = pl.DeviceIdType.MESH
DIAGONAL = ((1, 1, 2), (1, 2, 1), (2, 1, 1), (2, 1, 1))


def product(left, right):
    return jnp.dot(left, right, preferred_element_type=jnp.float32)


def rows_product(left, right):
    return lax.dot_general(
        left, right, (((1,), (1,)), ((), ())), preferred_element_type=jnp.float32
    )


def kernel(
    doms, mps, square, shifts,
    node_h, edge_h, edge_w, send_w, receive_w, output_w, gain_h, send_h, receive_h, rows_h, node_g_h, edge_g_h,
    new_node_h, new_edge_h, grad_node_h, grad_edge_h,
    weights, node, edge, gain, sender, receiver, rows, node_g, edge_g,
    table, halo, back, returned, new_node, new_edge, grad_node, grad_edge,
    load_sem, store_sem, send_sem, recv_sem,
):
    dom, mp = lax.axis_index("dom"), lax.axis_index("mp")
    block = dom * mps + mp
    blocks = doms * mps
    count, halo_rows = node.shape[0], halo.shape[0] // len(shifts)
    panels = (send_w, receive_w, edge_w, output_w)
    size = send_w.shape[0]

    loads = []

    def load(source, target):
        copy = pltpu.make_async_copy(source, target, load_sem.at[len(loads)])
        copy.start()
        loads.append(copy)
        return copy

    own = pl.ds(pl.multiple_of(mp * size, size), size)
    load_panel = [load(panels[w], weights.at[w, own]) for w in range(4)]
    load_node = load(node_h, node)
    load_rows = load(rows_h, rows)
    load_sender = load(send_h, sender)
    load_receiver = load(receive_h, receiver)
    load_edge = load(edge_h, edge)
    load_gain = load(gain_h, gain)
    load_node_g = load(node_g_h, node_g)
    load_edge_g = load(edge_g_h, edge_g)

    def at_block(offset):
        other = lax.rem(block + offset + blocks, blocks)
        return (lax.div(other, mps), lax.rem(other, mps))

    if square:
        x, deep = lax.rem(dom, 2), lax.rem(lax.div(dom, 2), 2)
        core, y = lax.rem(mp, 2), lax.div(mp, 2)
        twin = (dom, mp + 1 - 2 * core)
        over_y = (dom, mp + 2 - 4 * y)
        over_x = (dom + 1 - 2 * x, mp)
        over_z = (dom + 2 - 4 * deep, mp)
        peers = [twin, over_y, over_x, over_z]
    else:
        peers = [(dom, lax.rem(mp + step, mps)) for step in range(1, mps)]
    barrier = pltpu.get_barrier_semaphore()
    greeted = peers + [at_block(shift) for shift in shifts]
    for peer in greeted:
        pl.semaphore_signal(barrier, inc=1, device_id=peer, device_id_type=MESH)
    pl.semaphore_wait(barrier, len(greeted))

    sent = []

    def send(source, target, peer):
        index = len(sent)
        copy = pltpu.make_async_remote_copy(
            src_ref=source, dst_ref=target, send_sem=send_sem.at[index], recv_sem=recv_sem.at[index],
            device_id=peer, device_id_type=MESH,
        )
        copy.start()
        sent.append(copy)
        return copy

    if square:
        unit = size // 16
        quarter = size // 4
        mine = x + 2 * deep
        by_x, by_z, opposite = mine + 1 - 2 * x, mine + 2 - 4 * deep, 3 - mine
        far = (mp + 2 - 4 * y) * size
        near = mp * size

        def part(w, base, start, length):
            return weights.at[w, pl.ds(pl.multiple_of(base + start, unit), length)]

        A, B, DY, X, Z, DX, DZ, SB, SX, SZ, SD = ([None] * 4 for _ in range(11))

        def begin_twin(w):
            A[w] = send(panels[w], weights.at[w, own], twin)

        def begin(w):
            B[w] = send(
                panels[w].at[pl.ds(pl.multiple_of(mine * quarter, quarter), quarter)],
                part(w, near, mine * quarter, quarter), over_y,
            )
            length = DIAGONAL[w][0] * unit
            DY[w] = send(
                panels[w].at[pl.ds(pl.multiple_of(opposite * quarter, quarter), length)],
                part(w, near, opposite * quarter, length), over_y,
            )

        def forward(w, start, length, peer):
            region = part(w, far, start, length)
            return send(region, region, peer)

        def step1(w):
            B[w].wait_recv()
            X[w] = forward(w, mine * quarter, quarter, over_x)
            Z[w] = forward(w, mine * quarter, quarter, over_z)
            SB[w] = forward(w, mine * quarter, quarter, twin)

        def step2(w):
            dy, dx, dz = (units * unit for units in DIAGONAL[w])
            X[w].wait_recv()
            DZ[w] = forward(w, by_x * quarter + dy + dx, dz, over_z)
            SX[w] = forward(w, by_x * quarter, quarter, twin)
            Z[w].wait_recv()
            DX[w] = forward(w, by_z * quarter + dy, dx, over_x)
            SZ[w] = forward(w, by_z * quarter, quarter, twin)

        def step3(w):
            DY[w].wait_recv()
            DX[w].wait_recv()
            DZ[w].wait_recv()
            SD[w] = forward(w, opposite * quarter, quarter, twin)

        def step4(w):
            load_panel[w].wait()
            for copy in (A[w], SB[w], SX[w], SZ[w], SD[w]):
                copy.wait_recv()
    else:
        direct = [[send(panels[w], weights.at[w, own], peer) for peer in peers] for w in range(4)]

        def step4(w):
            load_panel[w].wait()
            for copy in direct[w]:
                copy.wait_recv()

    def project_send():
        load_node.wait()
        load_rows.wait()
        table[:count] = product(node[...], weights[0]).astype(jnp.bfloat16)
        pick = (lax.broadcasted_iota(jnp.int32, (count, halo.shape[0]), 0) == rows[...]).astype(jnp.float32)
        halo[...] = product(pick.T.astype(jnp.bfloat16), table[:count]).astype(jnp.bfloat16)
        arrive = []
        for j, shift in enumerate(shifts):
            arrive.append(send(
                halo.at[pl.ds(j * halo_rows, halo_rows)],
                table.at[pl.ds(count + j * halo_rows, halo_rows)], at_block(shift),
            ))
        return pick.astype(jnp.bfloat16), arrive

    lookup_rows = count + halo.shape[0]

    def project_receive():
        table[lookup_rows:] = product(node[...], weights[1]).astype(jnp.bfloat16)

    if square:
        for w in range(4):
            begin_twin(w)
        begin(0)
        begin(1)
        step1(0)
        begin(2)
        step2(0)
        step1(1)
        begin(3)
        step3(0)
        step2(1)
        step4(0)
        pick, arrive = project_send()
        step1(2)
        step3(1)
        step2(2)
        step4(1)
        project_receive()
        step1(3)
        step3(2)
        step2(3)
        step4(2)
    else:
        step4(0)
        pick, arrive = project_send()
        step4(1)
        project_receive()
        step4(2)

    for copy in (load_edge, load_sender, load_receiver, load_gain, load_node_g, load_edge_g):
        copy.wait()
    edges = edge.shape[0]
    by_sender = lax.broadcasted_iota(jnp.int32, (lookup_rows, edges), 0) == sender[...]
    by_receiver = lax.broadcasted_iota(jnp.int32, (count, edges), 0) == receiver[...]
    to_table = jnp.concatenate([by_sender.astype(jnp.float32), by_receiver.astype(jnp.float32)], axis=0)
    from_table = to_table.T.astype(jnp.bfloat16)
    to_receiver = by_receiver.astype(jnp.float32)
    from_receiver = to_receiver.T.astype(jnp.bfloat16)
    to_table = to_table.astype(jnp.bfloat16)
    to_receiver = to_receiver.astype(jnp.bfloat16)

    preact = product(edge[...], weights[2])
    if square:
        step3(3)
    grad_total = edge_g[...].astype(jnp.float32) + product(from_receiver, node_g[...])
    for copy in arrive:
        copy.wait_recv()
    preact = preact + product(from_table, table[...])
    sigmoid = jax.nn.sigmoid(preact)
    hidden = (preact * sigmoid).astype(jnp.bfloat16)
    slope = sigmoid * (1.0 + preact * (1.0 - sigmoid))
    scaled = grad_total * gain[...]

    step4(3)
    projected = product(hidden, weights[3])
    centred = projected - jnp.mean(projected, axis=-1, keepdims=True)
    variance = jnp.mean(centred * centred, axis=-1, keepdims=True)
    scale = lax.rsqrt(variance + eps)
    unit_rows = centred * scale
    new_edge[...] = (edge[...].astype(jnp.float32) + unit_rows * gain[...]).astype(jnp.bfloat16)

    stores = []

    def store(source, target):
        copy = pltpu.make_async_copy(source, target, store_sem.at[len(stores)])
        copy.start()
        stores.append(copy)

    store(new_edge, new_edge_h)
    along = jnp.mean(scaled * unit_rows, axis=-1, keepdims=True)
    grad_projected = scale * (scaled - jnp.mean(scaled, axis=-1, keepdims=True) - unit_rows * along)
    grad_hidden = rows_product(grad_projected.astype(jnp.bfloat16), weights[3])
    grad_preact = (grad_hidden * slope).astype(jnp.bfloat16)
    grad_table = product(to_table, grad_preact)
    back[...] = grad_table[count:lookup_rows].astype(jnp.bfloat16)
    home = []
    for j, shift in enumerate(shifts):
        piece = pl.ds(j * halo_rows, halo_rows)
        home.append(send(back.at[piece], returned.at[piece], at_block(-shift)))
    grad_edge[...] = (grad_total + rows_product(grad_preact, weights[2])).astype(jnp.bfloat16)
    store(grad_edge, grad_edge_h)
    new_node[...] = (node[...].astype(jnp.float32) + product(to_receiver, new_edge[...])).astype(jnp.bfloat16)
    store(new_node, new_node_h)
    grad_nodes = node_g[...].astype(jnp.float32) + rows_product(
        grad_table[lookup_rows:].astype(jnp.bfloat16), weights[1]
    )
    for copy in home:
        copy.wait_recv()
    grad_send = (grad_table[:count] + product(pick, returned[...])).astype(jnp.bfloat16)
    grad_node[...] = (grad_nodes + rows_product(grad_send, weights[0])).astype(jnp.bfloat16)
    store(grad_node, grad_node_h)
    for copy in sent:
        copy.wait_send()
    for copy in stores:
        copy.wait()


def solution(mesh):
    doms, mps = mesh.shape["dom"], mesh.shape["mp"]

    def shards(
        node_states, edge_states, edge_weight, send_weight, receive_weight, output_weight,
        norm_gain, senders, receivers, send_rows, node_cotangent, edge_cotangent,
    ):
        nodes, width = node_states.shape
        edges = edge_states.shape[0]
        hidden = edge_weight.shape[1]
        spread, halo_rows = send_rows.shape[1] // 2, send_rows.shape[2]
        halos = 2 * spread * halo_rows
        shifts = [step + 1 for step in range(spread)] + [-(step + 1) for step in range(spread)]
        square = mps == 4 and doms % 4 == 0 and edge_weight.shape[0] % 256 == 0
        copies = 4 * (13 if square else mps - 1) + 4 * spread
        any_space = pl.BlockSpec(memory_space=pl.ANY)
        bf16 = jnp.bfloat16
        return pl.pallas_call(
            functools.partial(kernel, doms, mps, square, shifts),
            out_shape=(
                jax.ShapeDtypeStruct((nodes, width), bf16),
                jax.ShapeDtypeStruct((edges, width), bf16),
                jax.ShapeDtypeStruct((nodes, width), bf16),
                jax.ShapeDtypeStruct((edges, width), bf16),
            ),
            in_specs=[any_space] * 12,
            out_specs=(any_space,) * 4,
            scratch_shapes=[
                pltpu.VMEM((4, width, hidden), bf16),
                pltpu.VMEM((nodes, width), bf16),
                pltpu.VMEM((edges, width), bf16),
                pltpu.VMEM((1, width), jnp.float32),
                pltpu.VMEM((1, edges), jnp.int32),
                pltpu.VMEM((1, edges), jnp.int32),
                pltpu.VMEM((1, halos), jnp.int32),
                pltpu.VMEM((nodes, width), bf16),
                pltpu.VMEM((edges, width), bf16),
                pltpu.VMEM((2 * nodes + halos, hidden), bf16),
                pltpu.VMEM((halos, hidden), bf16),
                pltpu.VMEM((halos, hidden), bf16),
                pltpu.VMEM((halos, hidden), bf16),
                pltpu.VMEM((nodes, width), bf16),
                pltpu.VMEM((edges, width), bf16),
                pltpu.VMEM((nodes, width), bf16),
                pltpu.VMEM((edges, width), bf16),
                pltpu.SemaphoreType.DMA((12,)),
                pltpu.SemaphoreType.DMA((4,)),
                pltpu.SemaphoreType.DMA((copies,)),
                pltpu.SemaphoreType.DMA((copies,)),
            ],
            compiler_params=pltpu.CompilerParams(
                collective_id=0, has_side_effects=True, vmem_limit_bytes=60 * 1024 * 1024
            ),
            cost_estimate=pl.CostEstimate(flops=2 * width * hidden * 4 * (nodes + edges), bytes_accessed=16 * width * hidden, transcendentals=edges * hidden),
        )(
            node_states, edge_states, edge_weight, send_weight, receive_weight, output_weight,
            norm_gain.reshape(1, width), senders.reshape(1, edges), receivers.reshape(1, edges),
            send_rows.reshape(1, halos), node_cotangent, edge_cotangent,
        )

    rows = P(("dom", "mp"), None)
    panel = P("mp", None)
    indices = P(("dom", "mp"))
    return jax.shard_map(
        shards,
        mesh=mesh,
        in_specs=(rows, rows, panel, panel, panel, panel, P(), indices, indices, P(("dom", "mp"), None, None), rows, rows),
        out_specs=(rows,) * 4,
        check_vma=False,
    )
```

time: 155 us -> 51.9 us (0.33)
  waiting for transfers between devices: 80.1 us -> 0 us
  Pallas kernels: 0 us -> 45 us
  other arithmetic: 22.4 us -> 0 us
  matrix products: 16.8 us -> 0 us
  between operations: 14.2 us -> 0.65 us
  starting transfers between devices: 13.4 us -> 0 us
    all_gather x4 -> x0, waiting for transfers between devices: 77.5 us -> none  [the longest x1 22.7 us: shards(): lax.all_gather(receive_weight, 'mp', axis=0, tiled=True)]
    pallas_call x0 -> x1, Pallas kernels: none -> 45 us  [shards(): pl.pallas_call(functools.partial(kernel, doms, mps, square, shifts), out_...]
    scatter-add x7 -> x0, other arithmetic: 17.9 us -> none  [the longest x4 9.63 us: shards(): grad_send.at[chosen_rows[block_index]].add(returned.astype(jnp.float32))]
    dot_general x8 -> x0, matrix products: 16.8 us -> none  [the longest x4 8.76 us: product(): return jnp.dot(left, right, preferred_element_type=jnp.float32)]
    ppermute x8 -> x0, starting transfers between devices: 13.2 us -> none  [shifted(): return lax.ppermute(value, axis, pairs)]
    gather x7 -> x0, local copies, waits for them, and re-layouts: 5.41 us -> none  [the longest x4 2.36 us: collect(): jnp.take(source, chosen_rows[block_index], axis=0)]
    unnamed x37 -> x10, local copies, waits for them, and re-layouts: 0.67 us -> 5.48 us
    unnamed x4 -> x0, waiting for transfers between devices: 2.58 us -> none
  transfers between devices with their start and end apart: 12 -> 0, of which waited for: 4 -> 0; matrix products, arithmetic and copies ran while one was open for 20% -> 0% of each run, Pallas kernels for 0% -> 0%
where the time goes in v1:
time: 51.9 us; the launch traced here: 51.7 us
  Pallas kernels  45 us (87%)
  local copies, waits for them, and re-layouts  6.07 us (12%)
  between operations  0.65 us (1%)
    pallas_call x1, Pallas kernels, shards(): pl.pallas_call(functools.partial(kernel, doms, mps, square, shifts), out_...  45 us
    unnamed x10, local copies, waits for them, and re-layouts  5.48 us

profile of v1, /device:TPU:0, one launch (start us, length us, event | category | flops | bytes accessed | tf_op | source)
XLA Modules:
  0.0 51.7 jit_solution(14960718108046250395)
XLA Ops:
  0.6 0.0 copy-start.2
  0.6 0.7 %copy-done.2 = s32[1,4,16]{2,1,0:T(4,128)S(1)} copy-done((s32[1,4,16]{2,1,0:T(4,128)S(1)}, s32[1,4,16]{2,1,0:T(4,128)}, u32[]{:S(2)}) %copy-start.2) | copy-done | bytes 280
  1.3 0.6 %reshape.23.rows_h = s32[1,64]{1,0:T(1,128)} reshape(s32[1,4,16]{2,1,0:T(4,128)S(1)} %copy-done.2) | data formatting | bytes 512 | tf_op jit(solution)/shard_map/reshape | solution.py:329
  1.9 45.0 %shard_map.147 = (bf16[64,1024]{1,0:T(8,128)(2,1)}, bf16[192,1024]{1,0:T(8,128)(2,1)}, bf16[64,1024]{1,0:T(8,128)(2,1)}, bf16[192,1024]{1,0:T(8,128)(2,1)}) custom-call(bf16[64,1024]{1,0:T(8,128)(2,1)} %node_h.1, bf16[192,1024]{1,0:T(8,128)(2,1)} %edge_h.1, bf16[256,1024]{1,0:T(8,128)(2,1)} %edge_w.1, bf16[256,1024]{1,0:T(8,128)(2,1)} %send_w.1, ...), custom_call_target="tpu_custom_call" | custom-call | flops 2147483648 | bytes 16777216 | tf_op jit(solution)/shard_map/pallas_call | solution.py:289
  46.9 1.6 %copy.20 = bf16[64,1024]{1,0:T(8,128)(2,1)} copy(bf16[64,1024]{1,0:T(8,128)(2,1)} %get-tuple-element.8) | data formatting | bytes 262144
  48.5 0.0 copy-start.1
  48.5 0.0 copy-start
  48.5 1.8 %copy.21 = bf16[192,1024]{1,0:T(8,128)(2,1)} copy(bf16[192,1024]{1,0:T(8,128)(2,1)} %get-tuple-element.9) | data formatting | bytes 786432
  50.3 0.0 copy-done.1
  50.3 0.7 %copy.22 = bf16[64,1024]{1,0:T(8,128)(2,1)} copy(bf16[64,1024]{1,0:T(8,128)(2,1)S(1)} %copy-done.1) | data formatting | bytes 262144
  51.0 0.0 copy-done
  51.0 0.7 %copy.23 = bf16[192,1024]{1,0:T(8,128)(2,1)} copy(bf16[192,1024]{1,0:T(8,128)(2,1)S(1)} %copy-done) | data formatting | bytes 786432
Async XLA Ops:
  0.6 0.7 %copy-start.2 = (s32[1,4,16]{2,1,0:T(4,128)S(1)}, s32[1,4,16]{2,1,0:T(4,128)}, u32[]{:S(2)}) copy-start(s32[1,4,16]{2,1,0:T(4,128)} %param.21) | copy-start | bytes 772
  48.5 1.8 %copy-start.1 = (bf16[64,1024]{1,0:T(8,128)(2,1)S(1)}, bf16[64,1024]{1,0:T(8,128)(2,1)}, u32[]{:S(2)}) copy-start(bf16[64,1024]{1,0:T(8,128)(2,1)} %get-tuple-element.10) | copy-start | bytes 393220
  48.5 2.5 %copy-start = (bf16[192,1024]{1,0:T(8,128)(2,1)S(1)}, bf16[192,1024]{1,0:T(8,128)(2,1)}, u32[]{:S(2)}) copy-start(bf16[192,1024]{1,0:T(8,128)(2,1)} %get-tuple-element.11) | copy-start | bytes 1179652

commit v2 on v1

--- a/solution.py
+++ b/solution.py
@@ -28,6 +28,7 @@
     new_node_h, new_edge_h, grad_node_h, grad_edge_h,
     weights, node, edge, gain, sender, receiver, rows, node_g, edge_g,
     table, halo, back, returned, new_node, new_edge, grad_node, grad_edge,
+    wide, slope, grad_total, scaled, hidden, grad_projected, grad_preact,
     load_sem, store_sem, send_sem, recv_sem,
 ):
     dom, mp = lax.axis_index("dom"), lax.axis_index("mp")
@@ -109,6 +110,8 @@
                 panels[w].at[pl.ds(pl.multiple_of(mine * quarter, quarter), quarter)],
                 part(w, near, mine * quarter, quarter), over_y,
             )
+
+        def begin_diagonal(w):
             length = DIAGONAL[w][0] * unit
             DY[w] = send(
                 panels[w].at[pl.ds(pl.multiple_of(opposite * quarter, quarter), length)],
@@ -123,6 +126,12 @@
             B[w].wait_recv()
             X[w] = forward(w, mine * quarter, quarter, over_x)
             Z[w] = forward(w, mine * quarter, quarter, over_z)
+            if w < 2:
+                begin(w + 2)
+                begin_diagonal(w)
+            elif w == 2:
+                begin_diagonal(2)
+                begin_diagonal(3)
             SB[w] = forward(w, mine * quarter, quarter, twin)
 
         def step2(w):
@@ -155,8 +164,9 @@
     def project_send():
         load_node.wait()
         load_rows.wait()
+        chosen = jnp.concatenate([rows[0, j : j + 1, :] for j in range(len(shifts))], axis=1)
         table[:count] = product(node[...], weights[0]).astype(jnp.bfloat16)
-        pick = (lax.broadcasted_iota(jnp.int32, (count, halo.shape[0]), 0) == rows[...]).astype(jnp.float32)
+        pick = (lax.broadcasted_iota(jnp.int32, (count, halo.shape[0]), 0) == chosen).astype(jnp.float32)
         halo[...] = product(pick.T.astype(jnp.bfloat16), table[:count]).astype(jnp.bfloat16)
         arrive = []
         for j, shift in enumerate(shifts):
@@ -172,27 +182,28 @@
         table[lookup_rows:] = product(node[...], weights[1]).astype(jnp.bfloat16)
 
     if square:
-        for w in range(4):
-            begin_twin(w)
         begin(0)
         begin(1)
+        begin_twin(0)
+        begin_twin(1)
         step1(0)
-        begin(2)
+        begin_twin(2)
+        step1(1)
+        begin_twin(3)
         step2(0)
-        step1(1)
-        begin(3)
+        step1(2)
+        step2(1)
         step3(0)
-        step2(1)
+        step1(3)
+        step2(2)
+        step3(1)
         step4(0)
         pick, arrive = project_send()
-        step1(2)
-        step3(1)
-        step2(2)
+        step2(3)
+        step3(2)
         step4(1)
         project_receive()
-        step1(3)
-        step3(2)
-        step2(3)
+        step3(3)
         step4(2)
     else:
         step4(0)
@@ -213,25 +224,32 @@
     to_table = to_table.astype(jnp.bfloat16)
     to_receiver = to_receiver.astype(jnp.bfloat16)
 
-    preact = product(edge[...], weights[2])
-    if square:
-        step3(3)
-    grad_total = edge_g[...].astype(jnp.float32) + product(from_receiver, node_g[...])
+    strips = [pl.ds(start, 16) for start in range(0, edges, 16)]
+    grad_total[...] = edge_g[...].astype(jnp.float32) + product(from_receiver, node_g[...])
+    for strip in strips:
+        values = grad_total[strip] * gain[...]
+        scaled[strip] = values - jnp.mean(values, axis=-1, keepdims=True)
+    wide[...] = product(edge[...], weights[2])
     for copy in arrive:
         copy.wait_recv()
-    preact = preact + product(from_table, table[...])
-    sigmoid = jax.nn.sigmoid(preact)
-    hidden = (preact * sigmoid).astype(jnp.bfloat16)
-    slope = sigmoid * (1.0 + preact * (1.0 - sigmoid))
-    scaled = grad_total * gain[...]
+    wide[...] += product(from_table, table[...])
+    for strip in strips:
+        values = wide[strip]
+        sigmoid = jax.nn.sigmoid(values)
+        hidden[strip] = (values * sigmoid).astype(jnp.bfloat16)
+        slope[strip] = sigmoid * (1.0 + values * (1.0 - sigmoid))
 
     step4(3)
-    projected = product(hidden, weights[3])
-    centred = projected - jnp.mean(projected, axis=-1, keepdims=True)
-    variance = jnp.mean(centred * centred, axis=-1, keepdims=True)
-    scale = lax.rsqrt(variance + eps)
-    unit_rows = centred * scale
-    new_edge[...] = (edge[...].astype(jnp.float32) + unit_rows * gain[...]).astype(jnp.bfloat16)
+    wide[...] = product(hidden[...], weights[3])
+    for strip in strips:
+        values = wide[strip]
+        centred = values - jnp.mean(values, axis=-1, keepdims=True)
+        variance = jnp.mean(centred * centred, axis=-1, keepdims=True)
+        along = jnp.mean(scaled[strip] * centred, axis=-1, keepdims=True)
+        scale = lax.rsqrt(variance + eps)
+        unit_rows = centred * scale
+        new_edge[strip] = (edge[strip].astype(jnp.float32) + unit_rows * gain[...]).astype(jnp.bfloat16)
+        grad_projected[strip] = (scale * (scaled[strip] - unit_rows * (scale * along))).astype(jnp.bfloat16)
 
     stores = []
 
@@ -241,17 +259,16 @@
         stores.append(copy)
 
     store(new_edge, new_edge_h)
-    along = jnp.mean(scaled * unit_rows, axis=-1, keepdims=True)
-    grad_projected = scale * (scaled - jnp.mean(scaled, axis=-1, keepdims=True) - unit_rows * along)
-    grad_hidden = rows_product(grad_projected.astype(jnp.bfloat16), weights[3])
-    grad_preact = (grad_hidden * slope).astype(jnp.bfloat16)
-    grad_table = product(to_table, grad_preact)
+    wide[...] = rows_product(grad_projected[...], weights[3])
+    for strip in strips:
+        grad_preact[strip] = (wide[strip] * slope[strip]).astype(jnp.bfloat16)
+    grad_table = product(to_table, grad_preact[...])
     back[...] = grad_table[count:lookup_rows].astype(jnp.bfloat16)
     home = []
     for j, shift in enumerate(shifts):
         piece = pl.ds(j * halo_rows, halo_rows)
         home.append(send(back.at[piece], returned.at[piece], at_block(-shift)))
-    grad_edge[...] = (grad_total + rows_product(grad_preact, weights[2])).astype(jnp.bfloat16)
+    grad_edge[...] = (grad_total[...] + rows_product(grad_preact[...], weights[2])).astype(jnp.bfloat16)
     store(grad_edge, grad_edge_h)
     new_node[...] = (node[...].astype(jnp.float32) + product(to_receiver, new_edge[...])).astype(jnp.bfloat16)
     store(new_node, new_node_h)
@@ -269,6 +286,14 @@
         copy.wait()
 
 
+def hand_out(*refs):
+    copies = [pltpu.make_async_copy(refs[i], refs[4 + i], refs[8].at[i]) for i in range(4)]
+    for copy in copies:
+        copy.start()
+    for copy in copies:
+        copy.wait()
+
+
 def solution(mesh):
     doms, mps = mesh.shape["dom"], mesh.shape["mp"]
 
@@ -286,7 +311,7 @@
         copies = 4 * (13 if square else mps - 1) + 4 * spread
         any_space = pl.BlockSpec(memory_space=pl.ANY)
         bf16 = jnp.bfloat16
-        return pl.pallas_call(
+        results = pl.pallas_call(
             functools.partial(kernel, doms, mps, square, shifts),
             out_shape=(
                 jax.ShapeDtypeStruct((nodes, width), bf16),
@@ -294,7 +319,7 @@
                 jax.ShapeDtypeStruct((nodes, width), bf16),
                 jax.ShapeDtypeStruct((edges, width), bf16),
             ),
-            in_specs=[any_space] * 12,
+            in_specs=[pl.BlockSpec(memory_space=pltpu.HBM)] * 12,
             out_specs=(any_space,) * 4,
             scratch_shapes=[
                 pltpu.VMEM((4, width, hidden), bf16),
@@ -303,7 +328,7 @@
                 pltpu.VMEM((1, width), jnp.float32),
                 pltpu.VMEM((1, edges), jnp.int32),
                 pltpu.VMEM((1, edges), jnp.int32),
-                pltpu.VMEM((1, halos), jnp.int32),
+                pltpu.VMEM(send_rows.shape, jnp.int32),
                 pltpu.VMEM((nodes, width), bf16),
                 pltpu.VMEM((edges, width), bf16),
                 pltpu.VMEM((2 * nodes + halos, hidden), bf16),
@@ -314,6 +339,13 @@
                 pltpu.VMEM((edges, width), bf16),
                 pltpu.VMEM((nodes, width), bf16),
                 pltpu.VMEM((edges, width), bf16),
+                pltpu.VMEM((edges, hidden), jnp.float32),
+                pltpu.VMEM((edges, hidden), jnp.float32),
+                pltpu.VMEM((edges, width), jnp.float32),
+                pltpu.VMEM((edges, width), jnp.float32),
+                pltpu.VMEM((edges, hidden), bf16),
+                pltpu.VMEM((edges, width), bf16),
+                pltpu.VMEM((edges, hidden), bf16),
                 pltpu.SemaphoreType.DMA((12,)),
                 pltpu.SemaphoreType.DMA((4,)),
                 pltpu.SemaphoreType.DMA((copies,)),
@@ -326,8 +358,15 @@
         )(
             node_states, edge_states, edge_weight, send_weight, receive_weight, output_weight,
             norm_gain.reshape(1, width), senders.reshape(1, edges), receivers.reshape(1, edges),
-            send_rows.reshape(1, halos), node_cotangent, edge_cotangent,
+            send_rows, node_cotangent, edge_cotangent,
         )
+        return pl.pallas_call(
+            hand_out,
+            out_shape=tuple(jax.ShapeDtypeStruct(result.shape, bf16) for result in results),
+            in_specs=[any_space] * 4,
+            out_specs=(any_space,) * 4,
+            scratch_shapes=[pltpu.SemaphoreType.DMA((4,))],
+        )(*results)
 
     rows = P(("dom", "mp"), None)
     panel = P("mp", None)

time: 51.9 us -> 74.6 us (1.44)
  Pallas kernels: 45 us -> 73.8 us
  local copies, waits for them, and re-layouts: 6.07 us -> 0 us
    pallas_call x0 -> x1, Pallas kernels: none -> 32.9 us  [shards(): pl.pallas_call(hand_out, out_shape=tuple((jax.ShapeDtypeStruct(result.sha...]
    unnamed x10 -> x0, local copies, waits for them, and re-layouts: 5.48 us -> none
    pallas_call x1, Pallas kernels: 45 us -> 40.9 us  [shards(): pl.pallas_call(functools.partial(kernel, doms, mps, square, shifts), out_...]
where the time goes in v2:
time: 74.6 us; the launch traced here: 74.4 us
  Pallas kernels  73.8 us (99%)
    pallas_call x1, Pallas kernels, shards(): pl.pallas_call(functools.partial(kernel, doms, mps, square, shifts), out_...  40.9 us
    pallas_call x1, Pallas kernels, shards(): pl.pallas_call(hand_out, out_shape=tuple((jax.ShapeDtypeStruct(result.sha...  32.9 us

profile of v2, /device:TPU:0, one launch (start us, length us, event | category | flops | bytes accessed | tf_op | source)
XLA Modules:
  0.0 74.4 jit_solution(7381798660107332175)
XLA Ops:
  0.6 40.9 %shard_map.147 = (bf16[64,1024]{1,0:T(8,128)(2,1)}, bf16[192,1024]{1,0:T(8,128)(2,1)}, bf16[64,1024]{1,0:T(8,128)(2,1)}, bf16[192,1024]{1,0:T(8,128)(2,1)}) custom-call(bf16[64,1024]{1,0:T(8,128)(2,1)} %node_h.1, bf16[192,1024]{1,0:T(8,128)(2,1)} %edge_h.1, bf16[256,1024]{1,0:T(8,128)(2,1)} %edge_w.1, bf16[256,1024]{1,0:T(8,128)(2,1)} %send_w.1, ...), custom_call_target="tpu_custom_call" | custom-call | flops 2147483648 | bytes 16777216 | tf_op jit(solution)/shard_map/pallas_call | solution.py:314
  41.5 32.9 %shard_map.148 = (bf16[64,1024]{1,0:T(8,128)(2,1)}, bf16[192,1024]{1,0:T(8,128)(2,1)}, bf16[64,1024]{1,0:T(8,128)(2,1)}, bf16[192,1024]{1,0:T(8,128)(2,1)}) custom-call(bf16[64,1024]{1,0:T(8,128)(2,1)} %get-tuple-element.8.refs_0_, bf16[192,1024]{1,0:T(8,128)(2,1)} %get-tuple-element.9.refs_1_, bf16[64,1024]{1,0:T(8,128)(2,1)} %get-tuple-element.10.refs_2_, ...), custom_call_target="tpu_custom_call" | custom-call | tf_op jit(solution)/shard_map/pallas_call | solution.py:363

commit v3 on v2

--- a/solution.py
+++ b/solution.py
@@ -9,7 +9,7 @@
 
 eps = 1e-05
 MESH = pl.DeviceIdType.MESH
-DIAGONAL = ((1, 1, 2), (1, 2, 1), (2, 1, 1), (2, 1, 1))
+DIAGONAL = ((0, 2, 2), (0, 2, 2), (4, 0, 0), (4, 0, 0))
 
 
 def product(left, right):
@@ -25,17 +25,17 @@
 def kernel(
     doms, mps, square, shifts,
     node_h, edge_h, edge_w, send_w, receive_w, output_w, gain_h, send_h, receive_h, rows_h, node_g_h, edge_g_h,
-    new_node_h, new_edge_h, grad_node_h, grad_edge_h,
+    new_node, new_edge, grad_node, grad_edge,
     weights, node, edge, gain, sender, receiver, rows, node_g, edge_g,
-    table, halo, back, returned, new_node, new_edge, grad_node, grad_edge,
+    table, halo, back, returned,
     wide, slope, grad_total, scaled, hidden, grad_projected, grad_preact,
-    load_sem, store_sem, send_sem, recv_sem,
+    load_sem, send_sem, recv_sem,
 ):
     dom, mp = lax.axis_index("dom"), lax.axis_index("mp")
     block = dom * mps + mp
     blocks = doms * mps
     count, halo_rows = node.shape[0], halo.shape[0] // len(shifts)
-    panels = (send_w, receive_w, edge_w, output_w)
+    panels = (send_w, edge_w, receive_w, output_w)
     size = send_w.shape[0]
 
     loads = []
@@ -126,27 +126,29 @@
             B[w].wait_recv()
             X[w] = forward(w, mine * quarter, quarter, over_x)
             Z[w] = forward(w, mine * quarter, quarter, over_z)
-            if w < 2:
-                begin(w + 2)
+            if w == 0:
+                begin(2)
+            elif w == 1:
+                begin(3)
+            else:
                 begin_diagonal(w)
-            elif w == 2:
-                begin_diagonal(2)
-                begin_diagonal(3)
             SB[w] = forward(w, mine * quarter, quarter, twin)
 
         def step2(w):
             dy, dx, dz = (units * unit for units in DIAGONAL[w])
             X[w].wait_recv()
-            DZ[w] = forward(w, by_x * quarter + dy + dx, dz, over_z)
+            if dz:
+                DZ[w] = forward(w, by_x * quarter + dy + dx, dz, over_z)
             SX[w] = forward(w, by_x * quarter, quarter, twin)
             Z[w].wait_recv()
-            DX[w] = forward(w, by_z * quarter + dy, dx, over_x)
+            if dx:
+                DX[w] = forward(w, by_z * quarter + dy, dx, over_x)
             SZ[w] = forward(w, by_z * quarter, quarter, twin)
 
         def step3(w):
-            DY[w].wait_recv()
-            DX[w].wait_recv()
-            DZ[w].wait_recv()
+            for copy in (DY[w], DX[w], DZ[w]):
+                if copy is not None:
+                    copy.wait_recv()
             SD[w] = forward(w, opposite * quarter, quarter, twin)
 
         def step4(w):
@@ -179,39 +181,13 @@
     lookup_rows = count + halo.shape[0]
 
     def project_receive():
-        table[lookup_rows:] = product(node[...], weights[1]).astype(jnp.bfloat16)
+        table[lookup_rows:] = product(node[...], weights[2]).astype(jnp.bfloat16)
 
     if square:
         begin(0)
         begin(1)
         begin_twin(0)
         begin_twin(1)
-        step1(0)
-        begin_twin(2)
-        step1(1)
-        begin_twin(3)
-        step2(0)
-        step1(2)
-        step2(1)
-        step3(0)
-        step1(3)
-        step2(2)
-        step3(1)
-        step4(0)
-        pick, arrive = project_send()
-        step2(3)
-        step3(2)
-        step4(1)
-        project_receive()
-        step3(3)
-        step4(2)
-    else:
-        step4(0)
-        pick, arrive = project_send()
-        step4(1)
-        project_receive()
-        step4(2)
-
     for copy in (load_edge, load_sender, load_receiver, load_gain, load_node_g, load_edge_g):
         copy.wait()
     edges = edge.shape[0]
@@ -229,7 +205,34 @@
     for strip in strips:
         values = grad_total[strip] * gain[...]
         scaled[strip] = values - jnp.mean(values, axis=-1, keepdims=True)
-    wide[...] = product(edge[...], weights[2])
+    if square:
+        step1(0)
+        begin_twin(2)
+        step1(1)
+        begin_twin(3)
+        step2(0)
+        step1(2)
+        step2(1)
+        step3(0)
+        step1(3)
+        step4(0)
+        pick, arrive = project_send()
+        step2(2)
+        step3(1)
+        step4(1)
+        wide[...] = product(edge[...], weights[1])
+        step3(2)
+        step2(3)
+        step3(3)
+        step4(2)
+    else:
+        step4(0)
+        pick, arrive = project_send()
+        step4(1)
+        wide[...] = product(edge[...], weights[1])
+        step4(2)
+    project_receive()
+
     for copy in arrive:
         copy.wait_recv()
     wide[...] += product(from_table, table[...])
@@ -251,14 +254,6 @@
         new_edge[strip] = (edge[strip].astype(jnp.float32) + unit_rows * gain[...]).astype(jnp.bfloat16)
         grad_projected[strip] = (scale * (scaled[strip] - unit_rows * (scale * along))).astype(jnp.bfloat16)
 
-    stores = []
-
-    def store(source, target):
-        copy = pltpu.make_async_copy(source, target, store_sem.at[len(stores)])
-        copy.start()
-        stores.append(copy)
-
-    store(new_edge, new_edge_h)
     wide[...] = rows_product(grad_projected[...], weights[3])
     for strip in strips:
         grad_preact[strip] = (wide[strip] * slope[strip]).astype(jnp.bfloat16)
@@ -268,22 +263,17 @@
     for j, shift in enumerate(shifts):
         piece = pl.ds(j * halo_rows, halo_rows)
         home.append(send(back.at[piece], returned.at[piece], at_block(-shift)))
-    grad_edge[...] = (grad_total[...] + rows_product(grad_preact[...], weights[2])).astype(jnp.bfloat16)
-    store(grad_edge, grad_edge_h)
+    grad_edge[...] = (grad_total[...] + rows_product(grad_preact[...], weights[1])).astype(jnp.bfloat16)
     new_node[...] = (node[...].astype(jnp.float32) + product(to_receiver, new_edge[...])).astype(jnp.bfloat16)
-    store(new_node, new_node_h)
     grad_nodes = node_g[...].astype(jnp.float32) + rows_product(
-        grad_table[lookup_rows:].astype(jnp.bfloat16), weights[1]
+        grad_table[lookup_rows:].astype(jnp.bfloat16), weights[2]
     )
     for copy in home:
         copy.wait_recv()
     grad_send = (grad_table[:count] + product(pick, returned[...])).astype(jnp.bfloat16)
     grad_node[...] = (grad_nodes + rows_product(grad_send, weights[0])).astype(jnp.bfloat16)
-    store(grad_node, grad_node_h)
     for copy in sent:
         copy.wait_send()
-    for copy in stores:
-        copy.wait()
 
 
 def hand_out(*refs):
@@ -314,13 +304,13 @@
         results = pl.pallas_call(
             functools.partial(kernel, doms, mps, square, shifts),
             out_shape=(
-                jax.ShapeDtypeStruct((nodes, width), bf16),
-                jax.ShapeDtypeStruct((edges, width), bf16),
-                jax.ShapeDtypeStruct((nodes, width), bf16),
-                jax.ShapeDtypeStruct((edges, width), bf16),
+                pltpu.VMEM((nodes, width), bf16),
+                pltpu.VMEM((edges, width), bf16),
+                pltpu.VMEM((nodes, width), bf16),
+                pltpu.VMEM((edges, width), bf16),
             ),
             in_specs=[pl.BlockSpec(memory_space=pltpu.HBM)] * 12,
-            out_specs=(any_space,) * 4,
+            out_specs=(pl.BlockSpec(memory_space=pltpu.VMEM),) * 4,
             scratch_shapes=[
                 pltpu.VMEM((4, width, hidden), bf16),
                 pltpu.VMEM((nodes, width), bf16),
@@ -335,10 +325,6 @@
                 pltpu.VMEM((halos, hidden), bf16),
                 pltpu.VMEM((halos, hidden), bf16),
                 pltpu.VMEM((halos, hidden), bf16),
-                pltpu.VMEM((nodes, width), bf16),
-                pltpu.VMEM((edges, width), bf16),
-                pltpu.VMEM((nodes, width), bf16),
-                pltpu.VMEM((edges, width), bf16),
                 pltpu.VMEM((edges, hidden), jnp.float32),
                 pltpu.VMEM((edges, hidden), jnp.float32),
                 pltpu.VMEM((edges, width), jnp.float32),
@@ -347,7 +333,6 @@
                 pltpu.VMEM((edges, width), bf16),
                 pltpu.VMEM((edges, hidden), bf16),
                 pltpu.SemaphoreType.DMA((12,)),
-                pltpu.SemaphoreType.DMA((4,)),
                 pltpu.SemaphoreType.DMA((copies,)),
                 pltpu.SemaphoreType.DMA((copies,)),
             ],

time: 74.6 us -> 73.8 us (0.989)
  Pallas kernels: 73.8 us -> 70.2 us
  local copies, waits for them, and re-layouts: 0 us -> 2.8 us
    pallas_call x1, Pallas kernels: 40.9 us -> 37.3 us  [shards(): pl.pallas_call(functools.partial(kernel, doms, mps, square, shifts), out_...]
    unnamed x0 -> x8, local copies, waits for them, and re-layouts: none -> 2.8 us
where the time goes in v3:
time: 73.8 us; the launch traced here: 73.7 us
  Pallas kernels  70.2 us (95%)
  local copies, waits for them, and re-layouts  2.8 us (4%)
    pallas_call x1, Pallas kernels, shards(): pl.pallas_call(functools.partial(kernel, doms, mps, square, shifts), out_...  37.3 us
    pallas_call x1, Pallas kernels, shards(): pl.pallas_call(hand_out, out_shape=tuple((jax.ShapeDtypeStruct(result.sha...  32.9 us
    unnamed x8, local copies, waits for them, and re-layouts  2.8 us

profile of v3, /device:TPU:0, one launch (start us, length us, event | category | flops | bytes accessed | tf_op | source)
XLA Modules:
  0.0 73.7 jit_solution(13259089649584490613)
XLA Ops:
  0.6 37.3 %shard_map.147 = (bf16[64,1024]{1,0:T(8,128)(2,1)S(1)}, bf16[192,1024]{1,0:T(8,128)(2,1)S(1)}, bf16[64,1024]{1,0:T(8,128)(2,1)S(1)}, bf16[192,1024]{1,0:T(8,128)(2,1)S(1)}) custom-call(bf16[64,1024]{1,0:T(8,128)(2,1)} %node_h.1, bf16[192,1024]{1,0:T(8,128)(2,1)} %edge_h.1, bf16[256,1024]{1,0:T(8,128)(2,1)} %edge_w.1, bf16[256,1024]{1,0:T(8,128)(2,1)} %send_w.1, ...), custom_call_target="tpu_custom_call" | custom-call | flops 2147483648 | bytes 16777216 | tf_op jit(solution)/shard_map/pallas_call | solution.py:304
  38.0 0.0 copy-start
  38.0 0.7 copy-done
  38.7 0.0 copy-start.1
  38.7 0.8 %copy-done.1 = bf16[192,1024]{1,0:T(8,128)(2,1)} copy-done((bf16[192,1024]{1,0:T(8,128)(2,1)}, bf16[192,1024]{1,0:T(8,128)(2,1)S(1)}, u32[]{:S(2)}) %copy-start.1) | copy-done | bytes 393240
  39.5 0.0 copy-start.2
  39.5 0.6 copy-done.2
  40.1 0.0 copy-start.3
  40.1 0.7 copy-done.3
  40.8 32.9 %shard_map.148 = (bf16[64,1024]{1,0:T(8,128)(2,1)}, bf16[192,1024]{1,0:T(8,128)(2,1)}, bf16[64,1024]{1,0:T(8,128)(2,1)}, bf16[192,1024]{1,0:T(8,128)(2,1)}) custom-call(bf16[64,1024]{1,0:T(8,128)(2,1)} %copy-done.2, bf16[192,1024]{1,0:T(8,128)(2,1)} %copy-done, bf16[64,1024]{1,0:T(8,128)(2,1)} %copy-done.3, bf16[192,1024]{1,0:T(8,128)(2,1)} %copy-done.1), custom_call_target="tpu_custom_call" | custom-call | tf_op jit(solution)/shard_map/pallas_call | solution.py:348
Async XLA Ops:
  38.0 0.7 %copy-start = (bf16[192,1024]{1,0:T(8,128)(2,1)}, bf16[192,1024]{1,0:T(8,128)(2,1)S(1)}, u32[]{:S(2)}) copy-start(bf16[192,1024]{1,0:T(8,128)(2,1)S(1)} %get-tuple-element.9.refs_1_) | copy-start | bytes 1179652
  38.7 0.8 %copy-start.1 = (bf16[192,1024]{1,0:T(8,128)(2,1)}, bf16[192,1024]{1,0:T(8,128)(2,1)S(1)}, u32[]{:S(2)}) copy-start(bf16[192,1024]{1,0:T(8,128)(2,1)S(1)} %get-tuple-element.11.refs_3_) | copy-start | bytes 1179652
  39.5 0.6 copy-start.2
  40.1 0.7 copy-start.3

commit v4 on v3

--- a/solution.py
+++ b/solution.py
@@ -9,7 +9,11 @@
 
 eps = 1e-05
 MESH = pl.DeviceIdType.MESH
-DIAGONAL = ((0, 2, 2), (0, 2, 2), (4, 0, 0), (4, 0, 0))
+OVER_Y = (
+    (0, True), (1, True), (2, True), (3, True), (4, True), (5, True),
+    (4, False), (5, False), (6, True), (7, True), (6, False), (7, False),
+)
+IN_FLIGHT = 3
 
 
 def product(left, right):
@@ -28,7 +32,7 @@
     new_node, new_edge, grad_node, grad_edge,
     weights, node, edge, gain, sender, receiver, rows, node_g, edge_g,
     table, halo, back, returned,
-    wide, slope, grad_total, scaled, hidden, grad_projected, grad_preact,
+    wide, grad_table, slope, grad_total, scaled, hidden, grad_projected, grad_preact,
     load_sem, send_sem, recv_sem,
 ):
     dom, mp = lax.axis_index("dom"), lax.axis_index("mp")
@@ -90,75 +94,76 @@
         return copy
 
     if square:
-        unit = size // 16
         quarter = size // 4
+        half = quarter // 2
         mine = x + 2 * deep
         by_x, by_z, opposite = mine + 1 - 2 * x, mine + 2 - 4 * deep, 3 - mine
         far = (mp + 2 - 4 * y) * size
         near = mp * size
 
-        def part(w, base, start, length):
-            return weights.at[w, pl.ds(pl.multiple_of(base + start, unit), length)]
-
-        A, B, DY, X, Z, DX, DZ, SB, SX, SZ, SD = ([None] * 4 for _ in range(11))
+        def part(w, start, length):
+            return weights.at[w, pl.ds(pl.multiple_of(start, 16), length)]
+
+        def place(piece, which):
+            return which * quarter + (piece % 2) * half
+
+        A = [None] * 4
+        Y = [None] * len(OVER_Y)
+        X, Z, DX, DZ, SB, SX, SZ, SD = ([None] * 8 for _ in range(8))
 
         def begin_twin(w):
             A[w] = send(panels[w], weights.at[w, own], twin)
 
-        def begin(w):
-            B[w] = send(
-                panels[w].at[pl.ds(pl.multiple_of(mine * quarter, quarter), quarter)],
-                part(w, near, mine * quarter, quarter), over_y,
+        def begin(step):
+            piece, direct = OVER_Y[step]
+            start = place(piece, mine if direct else opposite)
+            Y[step] = send(
+                panels[piece // 2].at[pl.ds(pl.multiple_of(start, 16), half)],
+                part(piece // 2, near + start, half), over_y,
             )
 
-        def begin_diagonal(w):
-            length = DIAGONAL[w][0] * unit
-            DY[w] = send(
-                panels[w].at[pl.ds(pl.multiple_of(opposite * quarter, quarter), length)],
-                part(w, near, opposite * quarter, length), over_y,
-            )
-
-        def forward(w, start, length, peer):
-            region = part(w, far, start, length)
+        def forward(piece, which, peer, start=0, length=half):
+            region = part(piece // 2, far + place(piece, which) + start, length)
             return send(region, region, peer)
 
-        def step1(w):
-            B[w].wait_recv()
-            X[w] = forward(w, mine * quarter, quarter, over_x)
-            Z[w] = forward(w, mine * quarter, quarter, over_z)
-            if w == 0:
-                begin(2)
-            elif w == 1:
-                begin(3)
+        def arrive_y(step):
+            piece, direct = OVER_Y[step]
+            Y[step].wait_recv()
+            if direct:
+                X[piece] = forward(piece, mine, over_x)
+                Z[piece] = forward(piece, mine, over_z)
+            if step + IN_FLIGHT < len(OVER_Y):
+                begin(step + IN_FLIGHT)
+            if direct:
+                SB[piece] = forward(piece, mine, twin)
             else:
-                begin_diagonal(w)
-            SB[w] = forward(w, mine * quarter, quarter, twin)
-
-        def step2(w):
-            dy, dx, dz = (units * unit for units in DIAGONAL[w])
-            X[w].wait_recv()
-            if dz:
-                DZ[w] = forward(w, by_x * quarter + dy + dx, dz, over_z)
-            SX[w] = forward(w, by_x * quarter, quarter, twin)
-            Z[w].wait_recv()
-            if dx:
-                DX[w] = forward(w, by_z * quarter + dy, dx, over_x)
-            SZ[w] = forward(w, by_z * quarter, quarter, twin)
-
-        def step3(w):
-            for copy in (DY[w], DX[w], DZ[w]):
-                if copy is not None:
+                SD[piece] = forward(piece, opposite, twin)
+
+        def arrive_plane(piece):
+            X[piece].wait_recv()
+            if piece < 4:
+                DZ[piece] = forward(piece, by_x, over_z, half // 2, half // 2)
+            SX[piece] = forward(piece, by_x, twin)
+            Z[piece].wait_recv()
+            if piece < 4:
+                DX[piece] = forward(piece, by_z, over_x, 0, half // 2)
+            SZ[piece] = forward(piece, by_z, twin)
+
+        def arrive_opposite(piece):
+            DX[piece].wait_recv()
+            DZ[piece].wait_recv()
+            SD[piece] = forward(piece, opposite, twin)
+
+        def complete(w):
+            load_panel[w].wait()
+            A[w].wait_recv()
+            for piece in (2 * w, 2 * w + 1):
+                for copy in (SB[piece], SX[piece], SZ[piece], SD[piece]):
                     copy.wait_recv()
-            SD[w] = forward(w, opposite * quarter, quarter, twin)
-
-        def step4(w):
-            load_panel[w].wait()
-            for copy in (A[w], SB[w], SX[w], SZ[w], SD[w]):
-                copy.wait_recv()
     else:
         direct = [[send(panels[w], weights.at[w, own], peer) for peer in peers] for w in range(4)]
 
-        def step4(w):
+        def complete(w):
             load_panel[w].wait()
             for copy in direct[w]:
                 copy.wait_recv()
@@ -184,8 +189,8 @@
         table[lookup_rows:] = product(node[...], weights[2]).astype(jnp.bfloat16)
 
     if square:
-        begin(0)
-        begin(1)
+        for step in range(IN_FLIGHT):
+            begin(step)
         begin_twin(0)
         begin_twin(1)
     for copy in (load_edge, load_sender, load_receiver, load_gain, load_node_g, load_edge_g):
@@ -205,45 +210,64 @@
     for strip in strips:
         values = grad_total[strip] * gain[...]
         scaled[strip] = values - jnp.mean(values, axis=-1, keepdims=True)
+    bands = [pl.ds(start, 256) for start in range(0, wide.shape[1], 256)]
+
+    def project_edge():
+        for band in bands:
+            wide[:, band] = product(edge[...], weights[1, :, band])
+
     if square:
-        step1(0)
+        arrive_y(0)
+        arrive_y(1)
         begin_twin(2)
-        step1(1)
+        arrive_plane(0)
+        arrive_y(2)
         begin_twin(3)
-        step2(0)
-        step1(2)
-        step2(1)
-        step3(0)
-        step1(3)
-        step4(0)
+        arrive_plane(1)
+        arrive_y(3)
+        arrive_opposite(0)
+        arrive_y(4)
+        arrive_plane(2)
+        arrive_opposite(1)
+        arrive_y(5)
+        arrive_plane(3)
+        complete(0)
         pick, arrive = project_send()
-        step2(2)
-        step3(1)
-        step4(1)
-        wide[...] = product(edge[...], weights[1])
-        step3(2)
-        step2(3)
-        step3(3)
-        step4(2)
+        arrive_opposite(2)
+        arrive_y(6)
+        arrive_plane(4)
+        arrive_opposite(3)
+        arrive_y(7)
+        arrive_plane(5)
+        arrive_y(8)
+        complete(1)
+        project_edge()
+        arrive_y(9)
+        arrive_y(10)
+        arrive_plane(6)
+        complete(2)
+        project_receive()
+        arrive_y(11)
+        arrive_plane(7)
     else:
-        step4(0)
+        complete(0)
         pick, arrive = project_send()
-        step4(1)
-        wide[...] = product(edge[...], weights[1])
-        step4(2)
-    project_receive()
+        complete(1)
+        project_edge()
+        complete(2)
+        project_receive()
 
     for copy in arrive:
         copy.wait_recv()
-    wide[...] += product(from_table, table[...])
-    for strip in strips:
-        values = wide[strip]
+    for band in bands:
+        values = wide[:, band] + product(from_table, table[:, band])
         sigmoid = jax.nn.sigmoid(values)
-        hidden[strip] = (values * sigmoid).astype(jnp.bfloat16)
-        slope[strip] = sigmoid * (1.0 + values * (1.0 - sigmoid))
-
-    step4(3)
-    wide[...] = product(hidden[...], weights[3])
+        hidden[:, band] = (values * sigmoid).astype(jnp.bfloat16)
+        slope[:, band] = sigmoid * (1.0 + values * (1.0 - sigmoid))
+
+    complete(3)
+    for band in bands:
+        wide[:, band] = product(hidden[...], weights[3, :, band])
     for strip in strips:
         values = wide[strip]
         centred = values - jnp.mean(values, axis=-1, keepdims=True)
@@ -254,16 +278,18 @@
         new_edge[strip] = (edge[strip].astype(jnp.float32) + unit_rows * gain[...]).astype(jnp.bfloat16)
         grad_projected[strip] = (scale * (scaled[strip] - unit_rows * (scale * along))).astype(jnp.bfloat16)
 
-    wide[...] = rows_product(grad_projected[...], weights[3])
-    for strip in strips:
-        grad_preact[strip] = (wide[strip] * slope[strip]).astype(jnp.bfloat16)
-    grad_table = product(to_table, grad_preact[...])
+    for band in bands:
+        values = rows_product(grad_projected[...], weights[3, band]) * slope[:, band]
+        grad_preact[:, band] = values.astype(jnp.bfloat16)
+        grad_table[:, band] = product(to_table, grad_preact[:, band])
     back[...] = grad_table[count:lookup_rows].astype(jnp.bfloat16)
     home = []
     for j, shift in enumerate(shifts):
         piece = pl.ds(j * halo_rows, halo_rows)
         home.append(send(back.at[piece], returned.at[piece], at_block(-shift)))
-    grad_edge[...] = (grad_total[...] + rows_product(grad_preact[...], weights[1])).astype(jnp.bfloat16)
+    for band in bands:
+        values = grad_total[:, band] + rows_product(grad_preact[...], weights[1, band])
+        grad_edge[:, band] = values.astype(jnp.bfloat16)
     new_node[...] = (node[...].astype(jnp.float32) + product(to_receiver, new_edge[...])).astype(jnp.bfloat16)
     grad_nodes = node_g[...].astype(jnp.float32) + rows_product(
         grad_table[lookup_rows:].astype(jnp.bfloat16), weights[2]
@@ -298,7 +324,7 @@
         halos = 2 * spread * halo_rows
         shifts = [step + 1 for step in range(spread)] + [-(step + 1) for step in range(spread)]
         square = mps == 4 and doms % 4 == 0 and edge_weight.shape[0] % 256 == 0
-        copies = 4 * (13 if square else mps - 1) + 4 * spread
+        copies = (72 if square else 4 * (mps - 1)) + 4 * spread
         any_space = pl.BlockSpec(memory_space=pl.ANY)
         bf16 = jnp.bfloat16
         results = pl.pallas_call(
@@ -326,6 +352,7 @@
                 pltpu.VMEM((halos, hidden), bf16),
                 pltpu.VMEM((halos, hidden), bf16),
                 pltpu.VMEM((edges, hidden), jnp.float32),
+                pltpu.VMEM((2 * nodes + halos, hidden), jnp.float32),
                 pltpu.VMEM((edges, hidden), jnp.float32),
                 pltpu.VMEM((edges, width), jnp.float32),
                 pltpu.VMEM((edges, width), jnp.float32),
@@ -348,9 +375,10 @@
         return pl.pallas_call(
             hand_out,
             out_shape=tuple(jax.ShapeDtypeStruct(result.shape, bf16) for result in results),
-            in_specs=[any_space] * 4,
+            in_specs=[pl.BlockSpec(memory_space=pltpu.VMEM)] * 4,
             out_specs=(any_space,) * 4,
             scratch_shapes=[pltpu.SemaphoreType.DMA((4,))],
+            compiler_params=pltpu.CompilerParams(vmem_limit_bytes=8 * 1024 * 1024),
         )(*results)
 
     rows = P(("dom", "mp"), None)

time: 73.8 us -> 42.1 us (0.57)
  Pallas kernels: 70.2 us -> 41.3 us
  local copies, waits for them, and re-layouts: 2.8 us -> 0 us
    pallas_call x1, Pallas kernels: 32.9 us -> 1 us  [shards(): pl.pallas_call(hand_out, out_shape=tuple((jax.ShapeDtypeStruct(result.sha...]
    pallas_call x1, Pallas kernels: 37.3 us -> 40.3 us  [shards(): pl.pallas_call(functools.partial(kernel, doms, mps, square, shifts), out_...]
    unnamed x8 -> x0, local copies, waits for them, and re-layouts: 2.8 us -> none
where the time goes in v4:
time: 42.1 us; the launch traced here: 41.9 us
  Pallas kernels  41.3 us (98%)
  between operations  0.64 us (2%)
    pallas_call x1, Pallas kernels, shards(): pl.pallas_call(functools.partial(kernel, doms, mps, square, shifts), out_...  40.3 us
    pallas_call x1, Pallas kernels, shards(): pl.pallas_call(hand_out, out_shape=tuple((jax.ShapeDtypeStruct(result.sha...  1 us

profile of v4, /device:TPU:0, one launch (start us, length us, event | category | flops | bytes accessed | tf_op | source)
XLA Modules:
  0.0 41.9 jit_solution(7654946128087068883)
XLA Ops:
  0.6 40.3 %shard_map.147 = (bf16[64,1024]{1,0:T(8,128)(2,1)S(1)}, bf16[192,1024]{1,0:T(8,128)(2,1)S(1)}, bf16[64,1024]{1,0:T(8,128)(2,1)S(1)}, bf16[192,1024]{1,0:T(8,128)(2,1)S(1)}) custom-call(bf16[64,1024]{1,0:T(8,128)(2,1)} %node_h.1, bf16[192,1024]{1,0:T(8,128)(2,1)} %edge_h.1, bf16[256,1024]{1,0:T(8,128)(2,1)} %edge_w.1, bf16[256,1024]{1,0:T(8,128)(2,1)} %send_w.1, ...), custom_call_target="tpu_custom_call" | custom-call | flops 2147483648 | bytes 16777216 | tf_op jit(solution)/shard_map/pallas_call | solution.py:330
  40.9 1.0 %shard_map.148 = (bf16[64,1024]{1,0:T(8,128)(2,1)}, bf16[192,1024]{1,0:T(8,128)(2,1)}, bf16[64,1024]{1,0:T(8,128)(2,1)}, bf16[192,1024]{1,0:T(8,128)(2,1)}) custom-call(bf16[64,1024]{1,0:T(8,128)(2,1)S(1)} %get-tuple-element.8.refs_0_, bf16[192,1024]{1,0:T(8,128)(2,1)S(1)} %get-tuple-element.9.refs_1_, bf16[64,1024]{1,0:T(8,128)(2,1)S(1)} %get-tuple-element.10.refs_2_, ...), custom_call_target="tpu_custom_call" | custom-call | tf_op jit(solution)/shard_map/pallas_call | solution.py:375

commit v5 on v3

--- a/solution.py
+++ b/solution.py
@@ -28,7 +28,7 @@
     new_node, new_edge, grad_node, grad_edge,
     weights, node, edge, gain, sender, receiver, rows, node_g, edge_g,
     table, halo, back, returned,
-    wide, slope, grad_total, scaled, hidden, grad_projected, grad_preact,
+    wide, grad_table, slope, grad_total, scaled, hidden, grad_projected, grad_preact,
     load_sem, send_sem, recv_sem,
 ):
     dom, mp = lax.axis_index("dom"), lax.axis_index("mp")
@@ -205,6 +205,12 @@
     for strip in strips:
         values = grad_total[strip] * gain[...]
         scaled[strip] = values - jnp.mean(values, axis=-1, keepdims=True)
+    bands = [pl.ds(start, 256) for start in range(0, wide.shape[1], 256)]
+
+    def project_edge():
+        for band in bands:
+            wide[:, band] = product(edge[...], weights[1, :, band])
+
     if square:
         step1(0)
         begin_twin(2)
@@ -220,30 +226,31 @@
         step2(2)
         step3(1)
         step4(1)
-        wide[...] = product(edge[...], weights[1])
+        project_edge()
         step3(2)
         step2(3)
         step3(3)
         step4(2)
+        project_receive()
     else:
         step4(0)
         pick, arrive = project_send()
         step4(1)
-        wide[...] = product(edge[...], weights[1])
+        project_edge()
         step4(2)
-    project_receive()
+        project_receive()
 
     for copy in arrive:
         copy.wait_recv()
-    wide[...] += product(from_table, table[...])
-    for strip in strips:
-        values = wide[strip]
+    for band in bands:
+        values = wide[:, band] + product(from_table, table[:, band])
         sigmoid = jax.nn.sigmoid(values)
-        hidden[strip] = (values * sigmoid).astype(jnp.bfloat16)
-        slope[strip] = sigmoid * (1.0 + values * (1.0 - sigmoid))
+        hidden[:, band] = (values * sigmoid).astype(jnp.bfloat16)
+        slope[:, band] = sigmoid * (1.0 + values * (1.0 - sigmoid))
 
     step4(3)
-    wide[...] = product(hidden[...], weights[3])
+    for band in bands:
+        wide[:, band] = product(hidden[...], weights[3, :, band])
     for strip in strips:
         values = wide[strip]
         centred = values - jnp.mean(values, axis=-1, keepdims=True)
@@ -254,16 +261,18 @@
         new_edge[strip] = (edge[strip].astype(jnp.float32) + unit_rows * gain[...]).astype(jnp.bfloat16)
         grad_projected[strip] = (scale * (scaled[strip] - unit_rows * (scale * along))).astype(jnp.bfloat16)
 
-    wide[...] = rows_product(grad_projected[...], weights[3])
-    for strip in strips:
-        grad_preact[strip] = (wide[strip] * slope[strip]).astype(jnp.bfloat16)
-    grad_table = product(to_table, grad_preact[...])
+    for band in bands:
+        values = rows_product(grad_projected[...], weights[3, band]) * slope[:, band]
+        grad_preact[:, band] = values.astype(jnp.bfloat16)
+        grad_table[:, band] = product(to_table, grad_preact[:, band])
     back[...] = grad_table[count:lookup_rows].astype(jnp.bfloat16)
     home = []
     for j, shift in enumerate(shifts):
         piece = pl.ds(j * halo_rows, halo_rows)
         home.append(send(back.at[piece], returned.at[piece], at_block(-shift)))
-    grad_edge[...] = (grad_total[...] + rows_product(grad_preact[...], weights[1])).astype(jnp.bfloat16)
+    for band in bands:
+        values = grad_total[:, band] + rows_product(grad_preact[...], weights[1, band])
+        grad_edge[:, band] = values.astype(jnp.bfloat16)
     new_node[...] = (node[...].astype(jnp.float32) + product(to_receiver, new_edge[...])).astype(jnp.bfloat16)
     grad_nodes = node_g[...].astype(jnp.float32) + rows_product(
         grad_table[lookup_rows:].astype(jnp.bfloat16), weights[2]
@@ -298,7 +307,7 @@
         halos = 2 * spread * halo_rows
         shifts = [step + 1 for step in range(spread)] + [-(step + 1) for step in range(spread)]
         square = mps == 4 and doms % 4 == 0 and edge_weight.shape[0] % 256 == 0
-        copies = 4 * (13 if square else mps - 1) + 4 * spread
+        copies = (38 if square else 4 * (mps - 1)) + 4 * spread
         any_space = pl.BlockSpec(memory_space=pl.ANY)
         bf16 = jnp.bfloat16
         results = pl.pallas_call(
@@ -326,6 +335,7 @@
                 pltpu.VMEM((halos, hidden), bf16),
                 pltpu.VMEM((halos, hidden), bf16),
                 pltpu.VMEM((edges, hidden), jnp.float32),
+                pltpu.VMEM((2 * nodes + halos, hidden), jnp.float32),
                 pltpu.VMEM((edges, hidden), jnp.float32),
                 pltpu.VMEM((edges, width), jnp.float32),
                 pltpu.VMEM((edges, width), jnp.float32),
@@ -348,9 +358,10 @@
         return pl.pallas_call(
             hand_out,
             out_shape=tuple(jax.ShapeDtypeStruct(result.shape, bf16) for result in results),
-            in_specs=[any_space] * 4,
+            in_specs=[pl.BlockSpec(memory_space=pltpu.VMEM)] * 4,
             out_specs=(any_space,) * 4,
             scratch_shapes=[pltpu.SemaphoreType.DMA((4,))],
+            compiler_params=pltpu.CompilerParams(vmem_limit_bytes=8 * 1024 * 1024),
         )(*results)
 
     rows = P(("dom", "mp"), None)

time: 73.8 us -> 39.8 us (0.54)
  Pallas kernels: 70.2 us -> 39 us
  local copies, waits for them, and re-layouts: 2.8 us -> 0 us
    pallas_call x1, Pallas kernels: 32.9 us -> 1 us  [shards(): pl.pallas_call(hand_out, out_shape=tuple((jax.ShapeDtypeStruct(result.sha...]
    unnamed x8 -> x0, local copies, waits for them, and re-layouts: 2.8 us -> none
where the time goes in v5:
time: 39.8 us; the launch traced here: 39.6 us
  Pallas kernels  39 us (98%)
  between operations  0.64 us (2%)
    pallas_call x1, Pallas kernels, shards(): pl.pallas_call(functools.partial(kernel, doms, mps, square, shifts), out_...  38 us
    pallas_call x1, Pallas kernels, shards(): pl.pallas_call(hand_out, out_shape=tuple((jax.ShapeDtypeStruct(result.sha...  1 us

profile of v5, /device:TPU:0, one launch (start us, length us, event | category | flops | bytes accessed | tf_op | source)
XLA Modules:
  0.0 39.6 jit_solution(9029819518034920028)
XLA Ops:
  0.6 38.0 %shard_map.147 = (bf16[64,1024]{1,0:T(8,128)(2,1)S(1)}, bf16[192,1024]{1,0:T(8,128)(2,1)S(1)}, bf16[64,1024]{1,0:T(8,128)(2,1)S(1)}, bf16[192,1024]{1,0:T(8,128)(2,1)S(1)}) custom-call(bf16[64,1024]{1,0:T(8,128)(2,1)} %node_h.1, bf16[192,1024]{1,0:T(8,128)(2,1)} %edge_h.1, bf16[256,1024]{1,0:T(8,128)(2,1)} %edge_w.1, bf16[256,1024]{1,0:T(8,128)(2,1)} %send_w.1, ...), custom_call_target="tpu_custom_call" | custom-call | flops 2147483648 | bytes 16777216 | tf_op jit(solution)/shard_map/pallas_call | solution.py:313
  38.6 1.0 %shard_map.148 = (bf16[64,1024]{1,0:T(8,128)(2,1)}, bf16[192,1024]{1,0:T(8,128)(2,1)}, bf16[64,1024]{1,0:T(8,128)(2,1)}, bf16[192,1024]{1,0:T(8,128)(2,1)}) custom-call(bf16[64,1024]{1,0:T(8,128)(2,1)S(1)} %get-tuple-element.8.refs_0_, bf16[192,1024]{1,0:T(8,128)(2,1)S(1)} %get-tuple-element.9.refs_1_, bf16[64,1024]{1,0:T(8,128)(2,1)S(1)} %get-tuple-element.10.refs_2_, ...), custom_call_target="tpu_custom_call" | custom-call | tf_op jit(solution)/shard_map/pallas_call | solution.py:358

commit v6 on v3

--- a/solution.py
+++ b/solution.py
@@ -132,29 +132,36 @@
                 begin(3)
             else:
                 begin_diagonal(w)
-            SB[w] = forward(w, mine * quarter, quarter, twin)
+            if w >= 2:
+                SB[w] = forward(w, mine * quarter, quarter, twin)
 
         def step2(w):
             dy, dx, dz = (units * unit for units in DIAGONAL[w])
             X[w].wait_recv()
             if dz:
                 DZ[w] = forward(w, by_x * quarter + dy + dx, dz, over_z)
-            SX[w] = forward(w, by_x * quarter, quarter, twin)
+            if w >= 2:
+                SX[w] = forward(w, by_x * quarter, quarter, twin)
             Z[w].wait_recv()
             if dx:
                 DX[w] = forward(w, by_z * quarter + dy, dx, over_x)
-            SZ[w] = forward(w, by_z * quarter, quarter, twin)
+            if w >= 2:
+                SZ[w] = forward(w, by_z * quarter, quarter, twin)
 
         def step3(w):
             for copy in (DY[w], DX[w], DZ[w]):
                 if copy is not None:
                     copy.wait_recv()
-            SD[w] = forward(w, opposite * quarter, quarter, twin)
+            if w >= 2:
+                SD[w] = forward(w, opposite * quarter, quarter, twin)
+            else:
+                SD[w] = forward(w, 0, size, twin)
 
         def step4(w):
             load_panel[w].wait()
             for copy in (A[w], SB[w], SX[w], SZ[w], SD[w]):
-                copy.wait_recv()
+                if copy is not None:
+                    copy.wait_recv()
     else:
         direct = [[send(panels[w], weights.at[w, own], peer) for peer in peers] for w in range(4)]
 
@@ -215,13 +222,13 @@
         step2(1)
         step3(0)
         step1(3)
+        step2(2)
         step4(0)
         pick, arrive = project_send()
-        step2(2)
         step3(1)
+        step3(2)
         step4(1)
         wide[...] = product(edge[...], weights[1])
-        step3(2)
         step2(3)
         step3(3)
         step4(2)
@@ -298,7 +305,7 @@
         halos = 2 * spread * halo_rows
         shifts = [step + 1 for step in range(spread)] + [-(step + 1) for step in range(spread)]
         square = mps == 4 and doms % 4 == 0 and edge_weight.shape[0] % 256 == 0
-        copies = 4 * (13 if square else mps - 1) + 4 * spread
+        copies = (32 if square else 4 * (mps - 1)) + 4 * spread
         any_space = pl.BlockSpec(memory_space=pl.ANY)
         bf16 = jnp.bfloat16
         results = pl.pallas_call(
@@ -348,9 +355,10 @@
         return pl.pallas_call(
             hand_out,
             out_shape=tuple(jax.ShapeDtypeStruct(result.shape, bf16) for result in results),
-            in_specs=[any_space] * 4,
+            in_specs=[pl.BlockSpec(memory_space=pltpu.VMEM)] * 4,
             out_specs=(any_space,) * 4,
             scratch_shapes=[pltpu.SemaphoreType.DMA((4,))],
+            compiler_params=pltpu.CompilerParams(vmem_limit_bytes=8 * 1024 * 1024),
         )(*results)
 
     rows = P(("dom", "mp"), None)

time: 73.8 us -> 38.8 us (0.53)
  Pallas kernels: 70.2 us -> 38 us
  local copies, waits for them, and re-layouts: 2.8 us -> 0 us
    pallas_call x1, Pallas kernels: 32.9 us -> 1 us  [shards(): pl.pallas_call(hand_out, out_shape=tuple((jax.ShapeDtypeStruct(result.sha...]
    unnamed x8 -> x0, local copies, waits for them, and re-layouts: 2.8 us -> none
where the time goes in v6:
time: 38.8 us; the launch traced here: 38.6 us
  Pallas kernels  38 us (98%)
  between operations  0.64 us (2%)
    pallas_call x1, Pallas kernels, shards(): pl.pallas_call(functools.partial(kernel, doms, mps, square, shifts), out_...  37 us
    pallas_call x1, Pallas kernels, shards(): pl.pallas_call(hand_out, out_shape=tuple((jax.ShapeDtypeStruct(result.sha...  1 us

profile of v6, /device:TPU:0, one launch (start us, length us, event | category | flops | bytes accessed | tf_op | source)
XLA Modules:
  0.0 38.6 jit_solution(11316153466355760093)
XLA Ops:
  0.6 37.0 %shard_map.147 = (bf16[64,1024]{1,0:T(8,128)(2,1)S(1)}, bf16[192,1024]{1,0:T(8,128)(2,1)S(1)}, bf16[64,1024]{1,0:T(8,128)(2,1)S(1)}, bf16[192,1024]{1,0:T(8,128)(2,1)S(1)}) custom-call(bf16[64,1024]{1,0:T(8,128)(2,1)} %node_h.1, bf16[192,1024]{1,0:T(8,128)(2,1)} %edge_h.1, bf16[256,1024]{1,0:T(8,128)(2,1)} %edge_w.1, bf16[256,1024]{1,0:T(8,128)(2,1)} %send_w.1, ...), custom_call_target="tpu_custom_call" | custom-call | flops 2147483648 | bytes 16777216 | tf_op jit(solution)/shard_map/pallas_call | solution.py:311
  37.6 1.0 %shard_map.148 = (bf16[64,1024]{1,0:T(8,128)(2,1)}, bf16[192,1024]{1,0:T(8,128)(2,1)}, bf16[64,1024]{1,0:T(8,128)(2,1)}, bf16[192,1024]{1,0:T(8,128)(2,1)}) custom-call(bf16[64,1024]{1,0:T(8,128)(2,1)S(1)} %get-tuple-element.8.refs_0_, bf16[192,1024]{1,0:T(8,128)(2,1)S(1)} %get-tuple-element.9.refs_1_, bf16[64,1024]{1,0:T(8,128)(2,1)S(1)} %get-tuple-element.10.refs_2_, ...), custom_call_target="tpu_custom_call" | custom-call | tf_op jit(solution)/shard_map/pallas_call | solution.py:355

commit v7 on v6

--- a/solution.py
+++ b/solution.py
@@ -158,8 +158,10 @@
                 SD[w] = forward(w, 0, size, twin)
 
         def step4(w):
-            load_panel[w].wait()
-            for copy in (A[w], SB[w], SX[w], SZ[w], SD[w]):
+            if w < 3:
+                load_panel[w].wait()
+                A[w].wait_recv()
+            for copy in (SB[w], SX[w], SZ[w], SD[w]):
                 if copy is not None:
                     copy.wait_recv()
     else:
@@ -249,8 +251,17 @@
         hidden[strip] = (values * sigmoid).astype(jnp.bfloat16)
         slope[strip] = sigmoid * (1.0 + values * (1.0 - sigmoid))
 
-    step4(3)
-    wide[...] = product(hidden[...], weights[3])
+    if square:
+        load_panel[3].wait()
+        A[3].wait_recv()
+        near_half = pl.ds(pl.multiple_of(y * 2 * size, 2 * size), 2 * size)
+        far_half = pl.ds(pl.multiple_of((1 - y) * 2 * size, 2 * size), 2 * size)
+        wide[...] = product(hidden[:, near_half], weights[3, near_half])
+        step4(3)
+        wide[...] += product(hidden[:, far_half], weights[3, far_half])
+    else:
+        step4(3)
+        wide[...] = product(hidden[...], weights[3])
     for strip in strips:
         values = wide[strip]
         centred = values - jnp.mean(values, axis=-1, keepdims=True)

time: 38.8 us -> 38.6 us (level)
  no operation moved by 1% of the time
where the time goes in v7:
time: 38.6 us; the launch traced here: 38.4 us
  Pallas kernels  37.8 us (98%)
  between operations  0.64 us (2%)
    pallas_call x1, Pallas kernels, shards(): pl.pallas_call(functools.partial(kernel, doms, mps, square, shifts), out_...  36.8 us
    pallas_call x1, Pallas kernels, shards(): pl.pallas_call(hand_out, out_shape=tuple((jax.ShapeDtypeStruct(result.sha...  1 us

profile of v7, /device:TPU:0, one launch (start us, length us, event | category | flops | bytes accessed | tf_op | source)
XLA Modules:
  0.0 38.4 jit_solution(14968486355370928852)
XLA Ops:
  0.6 36.8 %shard_map.147 = (bf16[64,1024]{1,0:T(8,128)(2,1)S(1)}, bf16[192,1024]{1,0:T(8,128)(2,1)S(1)}, bf16[64,1024]{1,0:T(8,128)(2,1)S(1)}, bf16[192,1024]{1,0:T(8,128)(2,1)S(1)}) custom-call(bf16[64,1024]{1,0:T(8,128)(2,1)} %node_h.1, bf16[192,1024]{1,0:T(8,128)(2,1)} %edge_h.1, bf16[256,1024]{1,0:T(8,128)(2,1)} %edge_w.1, bf16[256,1024]{1,0:T(8,128)(2,1)} %send_w.1, ...), custom_call_target="tpu_custom_call" | custom-call | flops 2147483648 | bytes 16777216 | tf_op jit(solution)/shard_map/pallas_call | solution.py:322
  37.4 1.0 %shard_map.148 = (bf16[64,1024]{1,0:T(8,128)(2,1)}, bf16[192,1024]{1,0:T(8,128)(2,1)}, bf16[64,1024]{1,0:T(8,128)(2,1)}, bf16[192,1024]{1,0:T(8,128)(2,1)}) custom-call(bf16[64,1024]{1,0:T(8,128)(2,1)S(1)} %get-tuple-element.8.refs_0_, bf16[192,1024]{1,0:T(8,128)(2,1)S(1)} %get-tuple-element.9.refs_1_, bf16[64,1024]{1,0:T(8,128)(2,1)S(1)} %get-tuple-element.10.refs_2_, ...), custom_call_target="tpu_custom_call" | custom-call | tf_op jit(solution)/shard_map/pallas_call | solution.py:366
